TPU v7x, 128 devices: a whole 4x4x4 slice. The times are simulated.
128 devices in a mesh: row: 16 (over x, y), col: 8 (over z, core).
Axes of the slice: x: 4, y: 4, z: 4, core: 2. Of those that a mesh axis runs over, the one named last changes fastest.
Arguments:
- features: float32 [384, 768, 256], P('row', 'col'), may hold values from -6 to 6
- depth_kernel: float32 [3, 3, 256], replicated, may hold values from -1.5 to 1.5
- value_weight: float32 [256, 256], replicated, may hold values from -0.375 to 0.375
- key_weight: float32 [256, 256], replicated, may hold values from -0.375 to 0.375
- centers: float32 [512, 256], replicated, may hold values from -6 to 6
- center_gain: float32 [256], replicated, may hold values from 0.1 to 1.9
- labels: int32 [384, 768], P('row', 'col'), may hold values from 0 to 511
- cotangent: float32 [384, 768, 512], P('row', 'col'), may hold values from -6 to 6
Outputs:
- new_centers: float32 [512, 256], replicated
- logits: float32 [384, 768, 512], P('row', 'col')
- grad_features: float32 [384, 768, 256], P('row', 'col')
- grad_centers: float32 [512, 256], replicated
- grad_value: float32 [256, 256], replicated
- grad_key: float32 [256, 256], replicated
All inputs are finite; a program needn't handle non-finite values.
Results may differ from a plain program's by a relative error of at most 0.00011.
Values sent between devices are 32-bit elements; how exact they have to be, the bound alone decides.
A program may use at most 64 MiB of HBM per device.

v0:
```python
import jax
import jax.numpy as jnp
from jax import lax
from jax.sharding import PartitionSpec as P


def padded_2(cells, sides, width):
    for axis, dim in sides:
        count = lax.axis_size(axis)
        ends = count - 1
        head = lax.slice_in_dim(cells, 0, width, axis=dim)
        tail = lax.slice_in_dim(cells, cells.shape[dim] - width, cells.shape[dim], axis=dim)
        cells = jnp.concatenate(
            [
                lax.ppermute(tail, axis, [(i, (i + 1) % count) for i in range(ends)]),
                cells,
                lax.ppermute(head, axis, [((i + 1) % count, i) for i in range(ends)]),
            ],
            axis=dim,
        )
    return cells


def matmul(left, right):
    return jnp.dot(left, right, preferred_element_type=jnp.float32, precision=lax.Precision.HIGHEST)


def inner_rows(left, right):
    return lax.dot_general(
        left,
        right,
        (((0,), (0,)), ((), ())),
        preferred_element_type=jnp.float32,
        precision=lax.Precision.HIGHEST,
    )


def normalize(sums):
    centred = sums - jnp.mean(sums, axis=1, keepdims=True)
    inverse = lax.rsqrt(jnp.mean(centred * centred, axis=1, keepdims=True) + 1e-05)
    return (centred * inverse, inverse)


def shards(
    features, depth_kernel, value_weight, key_weight, centers, center_gain, labels, cotangent
):
    rows, cols, chans = features.shape
    count = centers.shape[0]
    scale = 1.0 / jnp.sqrt(jnp.float32(chans))
    padded = padded_2(features, (("row", 0), ("col", 1)), 1)
    mixed = features
    for a in range(3):
        for b in range(3):
            mixed = mixed + depth_kernel[a, b] * padded[a : a + rows, b : b + cols]
    mixed = mixed.reshape(-1, chans)
    onehot = (labels.reshape(-1)[:, None] == lax.iota(jnp.int32, count)[None, :]).astype(
        jnp.float32
    )
    grads = cotangent.reshape(-1, count)
    by_label = inner_rows(onehot, mixed)
    by_grad = inner_rows(grads, mixed)
    by_label, by_grad = lax.psum((by_label, by_grad), ("row", "col"))
    sums = matmul(by_label, value_weight)
    normed, inverse = normalize(sums)
    new_centers = centers + center_gain * normed
    back = matmul(new_centers, key_weight.T) * scale
    logits = matmul(mixed, back.T)
    grad_centers = matmul(by_grad, key_weight) * scale
    grad_key = inner_rows(by_grad, new_centers) * scale
    dnorm = grad_centers * center_gain
    dsums = inverse * (
        dnorm
        - jnp.mean(dnorm, axis=1, keepdims=True)
        - normed * jnp.mean(dnorm * normed, axis=1, keepdims=True)
    )
    grad_value = inner_rows(by_label, dsums)
    dmixed = (matmul(onehot, matmul(dsums, value_weight.T)) + matmul(grads, back)).reshape(
        rows, cols, chans
    )
    rim = padded_2(dmixed, (("row", 0), ("col", 1)), 1)
    grad_features = dmixed
    for a in range(3):
        for b in range(3):
            grad_features = (
                grad_features + depth_kernel[a, b] * rim[2 - a : 2 - a + rows, 2 - b : 2 - b + cols]
            )
    return (
        new_centers,
        logits.reshape(rows, cols, count),
        grad_features,
        grad_centers,
        grad_value,
        grad_key,
    )


def solution(mesh):
    return jax.shard_map(
        shards,
        mesh=mesh,
        in_specs=(
            P("row", "col", None),
            P(),
            P(),
            P(),
            P(),
            P(),
            P("row", "col"),
            P("row", "col", None),
        ),
        out_specs=(P(), P("row", "col", None), P("row", "col", None), P(), P(), P()),
        check_vma=False,
    )
```

profile of v0, /device:TPU:1, one launch (start us, length us, event | category | flops | bytes accessed | tf_op | source)
XLA Modules:
  0.0 248.1 jit_solution(9860897988811860733)
XLA Ops:
  7.2 0.0 copy-start
  7.2 0.0 all-reduce.3.cloned.1.call-start
  7.2 1.0 fusion.42
  8.2 4.0 %collective-permute-start = (f32[1,96,256]{2,1,0:T(8,128)S(1)}, f32[1,96,256]{2,1,0:T(8,128)S(1)}, u32[]{:S(2)}, u32[]{:S(2)}) collective-permute-start(f32[1,96,256]{2,1,0:T(8,128)S(1)} %get-tuple-element.25), channel_id=1, source_target_pairs={{0,8},{8,16},{16,24},{24,32},{32,40},{40,48},{48,56},{56,64},{64,7... | collective-permute-start | bytes 294920 | tf_op jit(solution)/shard_map/ppermute | solution.py:15
  12.3 1.3 collective-permute-start.1
  13.6 0.3 collective-permute-done
  13.9 0.0 copy-start.10
  13.9 1.8 constant_dynamic-update-slice_fusion.1
  15.7 1.9 collective-permute-done.1
  17.6 0.0 copy-start.4
  17.6 1.5 copy-done.4
  19.1 5.5 %collective-permute-start.2 = (f32[26,1,256]{2,1,0:T(1,128)S(1)}, f32[26,1,256]{2,1,0:T(1,128)S(1)}, u32[]{:S(2)}, u32[]{:S(2)}) collective-permute-start(f32[26,1,256]{2,1,0:T(1,128)S(1)} %get-tuple-element.20), channel_id=1, source_target_pairs={{0,1},{1,2},{2,3},{3,4},{4,5},{5,6},{6,7},{8,9},{9,10},{10,11},{11... | collective-permute-start | bytes 79880 | tf_op jit(solution)/shard_map/ppermute | solution.py:15
  24.7 1.9 collective-permute-start.3
  26.6 0.0 copy-done.21
  26.6 0.0 copy-done.10
  26.7 0.0 copy-start.11
  26.7 0.0 copy-start.13
  26.7 0.0 copy-start.15
  26.7 0.0 copy-start.17
  26.7 0.0 copy-start.19
  26.7 0.1 eq.15
  26.8 0.0 collective-permute-done.2
  26.8 3.1 %collective-permute-done.3 = f32[26,1,256]{2,1,0:T(1,128)S(1)} collective-permute-done((f32[26,1,256]{2,1,0:T(1,128)S(1)}, f32[26,1,256]{2,1,0:T(1,128)S(1)}, u32[]{:S(2)}, u32[]{:S(2)}) %collective-permute-start.3) | collective-permute-done | bytes 26656 | tf_op jit(solution)/shard_map/ppermute | solution.py:17
  29.9 9.9 %fusion.8 = f32[24,96,256]{2,1,0:T(8,128)S(1)} fusion(f32[26,96,256]{2,1,0:T(8,128)} %copy-done.4, f32[24,96,256]{2,1,0:T(8,128)} %param.8, f32[26,1,256]{2,1,0:T(1,128)S(1)} %collective-permute-done.3, f32[26,1,256]{2,1,0:T(1,128)S(1)} %collective-permute-done.2, f32[1,96,256]{2,1,0:T(8,128)S(1)} %collective-permute-done.1, ...), kind=kLoop, calls=%fused_computation.20 | loop fusion | flops 15335424 | bytes 7533568 | tf_op jit(solution)/shard_map/add | solution.py:54
  39.8 0.0 copy-done.11
  39.8 0.0 copy-done.13
  39.8 0.0 copy-done.15
  39.8 0.0 copy-done.17
  39.8 0.0 copy-done.19
  39.8 0.0 copy-done.1
  39.8 4.9 %convolution_bitcast_fusion.1 = f32[512,256]{0,1:T(8,128)} fusion(f32[24,96,256]{2,1,0:T(8,128)S(1)} %fusion.8, f32[24,96,512]{2,1,0:T(8,128)S(1)} %copy-done.1), kind=kOutput, calls=%fused_computation.61 | convolution fusion | flops 3623878656 | bytes 7602176 | tf_op jit(solution)/shard_map/dot_general | solution.py:29
  44.8 5.0 %fusion.1 = f32[512,256]{1,0:T(8,128)} fusion(f32[2304,256]{1,0:T(8,128)S(1)} %bitcast.45, s32[2304]{0:T(1024)S(1)} %eq.15), kind=kOutput, calls=%fused_computation.2 | convolution fusion | flops 3625058304 | bytes 2892800 | tf_op jit(solution)/shard_map/dot_general | solution.py:29
  49.8 0.0 all-reduce.3.cloned.1.call-update
  49.8 1.0 copy.14
  50.8 149.4 %all-reduce.3.cloned.1.call-done = (f32[512,256]{1,0:T(8,128)}, f32[512,256]{0,1:T(8,128)}) async-done(((f32[512,256]{1,0:T(8,128)}, f32[512,256]{0,1:T(8,128)}), (f32[512,256]{1,0:T(8,128)}, f32[512,256]{0,1:T(8,128)})) %all-reduce.3.cloned.1.call-update) | async-done | bytes 1048592 | tf_op jit(solution)/shard_map/psum | solution.py:62
  200.2 1.8 fusion.44
  202.0 0.1 multiply_reduce_fusion.1
  202.1 2.0 multiply_reduce_fusion.2
  204.1 0.0 copy-start.2
  204.1 1.8 fusion.39
  205.9 1.3 fusion.40
  207.2 0.0 slice-start
  207.2 1.0 convolution_multiply_fusion
  208.3 0.0 slice-start.1
  208.3 5.5 %fusion.37 = f32[24,96,512]{2,1,0:T(8,128)} fusion(f32[24,96,256]{2,1,0:T(8,128)S(1)} %fusion.8, f32[512,256]{1,0:T(8,128)S(1)} %convolution_multiply_fusion), kind=kOutput, calls=%fused_computation.64 | convolution fusion | flops 3623878656 | bytes 7602176 | tf_op jit(solution)/shard_map/dot_general | solution.py:25
  213.8 0.0 slice-done.1
  213.8 4.3 %convolution_bitcast_fusion = f32[2304,256]{1,0:T(8,128)S(1)} fusion(f32[512,256]{1,0:T(8,128)S(1)} %convolution_multiply_fusion, f32[2304,512]{1,0:T(8,128)S(1)} %bitcast.48), kind=kOutput, calls=%fused_computation.4 | convolution fusion | flops 3623878656 | bytes 7602176 | tf_op jit(solution)/shard_map/dot_general | solution.py:25
  218.1 2.8 %fusion.2 = f32[2304,256]{1,0:T(8,128)S(1)} fusion(f32[2304,256]{1,0:T(8,128)S(1)} %convolution_bitcast_fusion, f32[512,256]{1,0:T(8,128)S(1)} %fusion.40, s32[2304]{0:T(1024)S(1)} %eq.15), kind=kOutput, calls=%fused_computation.3 | convolution fusion | flops 3625648128 | bytes 5252096 | tf_op jit(solution)/shard_map/dot_general | solution.py:25
  220.9 2.3 collective-permute-start.4
  223.2 1.3 collective-permute-start.5
  224.5 1.3 convolution_multiply_fusion.1
  225.9 1.0 copy.16
  226.9 0.0 collective-permute-done.4
  226.9 1.7 collective-permute-done.5
  228.6 4.1 %collective-permute-start.6 = (f32[26,1,256]{2,1,0:T(1,128)S(1)}, f32[26,1,256]{2,1,0:T(1,128)S(1)}, u32[]{:S(2)}, u32[]{:S(2)}) collective-permute-start(f32[26,1,256]{2,1,0:T(1,128)S(1)} %get-tuple-element.18), channel_id=1, source_target_pairs={{1,0},{2,1},{3,2},{4,3},{5,4},{6,5},{7,6},{9,8},{10,9},{11,10},{12... | collective-permute-start | bytes 79880 | tf_op jit(solution)/shard_map/ppermute | solution.py:17
  232.7 1.9 collective-permute-start.7
  234.6 0.8 broadcast_multiply_fusion
  235.5 1.0 copy.17
  236.5 0.0 collective-permute-done.6
  236.5 0.0 collective-permute-done.7
  236.5 0.5 pad_maximum_fusion
  237.0 0.1 copy-done.12
  237.1 0.0 copy-done.20
  237.2 4.1 %fusion.20 = f32[24,96,256]{2,1,0:T(8,128)} fusion(f32[26,97,256]{2,1,0:T(8,128)S(1)} %get-tuple-element.17, f32[24,96,256]{2,1,0:T(8,128)S(1)} %bitcast.44, f32[1,96,256]{2,1,0:T(8,128)S(1)} %collective-permute-done.4, f32[26,97,256]{2,1,0:T(8,128)S(1)} %get-tuple-element.16, f32[1,96,256]{2,1,0:T(8,128)S(1)} %collective-permute-done.5, ...), kind=kLoop, calls=%fused_computation.33 | loop fusion | flops 11796480 | bytes 19080192 | tf_op jit(solution)/shard_map/add | solution.py:85
  (38 shorter events, 0.2 us)
Async XLA Ops:
  7.2 195.0 %copy-start = (f32[256,256]{1,0:T(8,128)S(1)}, f32[256,256]{1,0:T(8,128)}, u32[]{:S(2)}) copy-start(f32[256,256]{1,0:T(8,128)} %param.11) | copy-start | bytes 786436
  7.2 193.0 %all-reduce.3.cloned.1.call-start = ((), (), s32[]{:S(2)}) async-start(), calls=%async_computation | async-start | bytes 2097152 | tf_op jit(solution)/shard_map/psum | solution.py:62
  8.2 5.7 %collective-permute-start = (f32[1,96,256]{2,1,0:T(8,128)S(1)}, f32[1,96,256]{2,1,0:T(8,128)S(1)}, u32[]{:S(2)}, u32[]{:S(2)}) collective-permute-start(f32[1,96,256]{2,1,0:T(8,128)S(1)} %get-tuple-element.25), channel_id=1, source_target_pairs={{0,8},{8,16},{16,24},{24,32},{32,40},{40,48},{48,56},{56,64},{64,7... | collective-permute-start | bytes 294920 | tf_op jit(solution)/shard_map/ppermute | solution.py:15
  12.3 5.4 %collective-permute-start.1 = (f32[1,96,256]{2,1,0:T(8,128)S(1)}, f32[1,96,256]{2,1,0:T(8,128)S(1)}, u32[]{:S(2)}, u32[]{:S(2)}) collective-permute-start(f32[1,96,256]{2,1,0:T(8,128)S(1)} %get-tuple-element.24), channel_id=1, source_target_pairs={{8,0},{16,8},{24,16},{32,24},{40,32},{48,40},{56,48},{64,56},{72,6... | collective-permute-start | bytes 294920 | tf_op jit(solution)/shard_map/ppermute | solution.py:17
  13.9 12.7 %copy-start.21 = (f32[3,3,256]{2,1,0:T(4,128)S(1)}, f32[3,3,256]{2,1,0:T(4,128)}, u32[]{:S(2)}) copy-start(f32[3,3,256]{2,1,0:T(4,128)} %param.9) | copy-start | bytes 27652
  13.9 12.8 %copy-start.10 = (s32[24,96]{1,0:T(8,128)S(1)}, s32[24,96]{1,0:T(8,128)}, u32[]{:S(2)}) copy-start(s32[24,96]{1,0:T(8,128)} %param.14) | copy-start | bytes 27652
  17.6 1.5 copy-start.4
  19.1 7.6 %collective-permute-start.2 = (f32[26,1,256]{2,1,0:T(1,128)S(1)}, f32[26,1,256]{2,1,0:T(1,128)S(1)}, u32[]{:S(2)}, u32[]{:S(2)}) collective-permute-start(f32[26,1,256]{2,1,0:T(1,128)S(1)} %get-tuple-element.20), channel_id=1, source_target_pairs={{0,1},{1,2},{2,3},{3,4},{4,5},{5,6},{6,7},{8,9},{9,10},{10,11},{11... | collective-permute-start | bytes 79880 | tf_op jit(solution)/shard_map/ppermute | solution.py:15
  24.7 5.2 %collective-permute-start.3 = (f32[26,1,256]{2,1,0:T(1,128)S(1)}, f32[26,1,256]{2,1,0:T(1,128)S(1)}, u32[]{:S(2)}, u32[]{:S(2)}) collective-permute-start(f32[26,1,256]{2,1,0:T(1,128)S(1)} %get-tuple-element.21), channel_id=1, source_target_pairs={{1,0},{2,1},{3,2},{4,3},{5,4},{6,5},{7,6},{9,8},{10,9},{11,10},{12... | collective-permute-start | bytes 79880 | tf_op jit(solution)/shard_map/ppermute | solution.py:17
  26.7 13.1 %copy-start.11 = (f32[1,1,256]{2,1,0:T(1,128)}, f32[1,1,256]{2,1,0:T(1,128)S(1)}, u32[]{:S(2)}) copy-start(f32[1,1,256]{2,1,0:T(1,128)S(1)} %get-tuple-element.31) | copy-start | bytes 3076
  26.7 13.1 %copy-start.13 = (f32[1,1,256]{2,1,0:T(1,128)}, f32[1,1,256]{2,1,0:T(1,128)S(1)}, u32[]{:S(2)}) copy-start(f32[1,1,256]{2,1,0:T(1,128)S(1)} %get-tuple-element.32) | copy-start | bytes 3076
  26.7 13.1 %copy-start.15 = (f32[1,1,256]{2,1,0:T(1,128)}, f32[1,1,256]{2,1,0:T(1,128)S(1)}, u32[]{:S(2)}) copy-start(f32[1,1,256]{2,1,0:T(1,128)S(1)} %get-tuple-element.33) | copy-start | bytes 3076
  26.7 13.1 %copy-start.17 = (f32[1,1,256]{2,1,0:T(1,128)}, f32[1,1,256]{2,1,0:T(1,128)S(1)}, u32[]{:S(2)}) copy-start(f32[1,1,256]{2,1,0:T(1,128)S(1)} %get-tuple-element.34) | copy-start | bytes 3076
  26.7 13.1 %copy-start.19 = (f32[1,1,256]{2,1,0:T(1,128)}, f32[1,1,256]{2,1,0:T(1,128)S(1)}, u32[]{:S(2)}) copy-start(f32[1,1,256]{2,1,0:T(1,128)S(1)} %get-tuple-element.35) | copy-start | bytes 3076
  29.9 9.9 %copy-start.1 = (f32[24,96,512]{2,1,0:T(8,128)S(1)}, f32[24,96,512]{2,1,0:T(8,128)}, u32[]{:S(2)}) copy-start(f32[24,96,512]{2,1,0:T(8,128)} %param.15) | copy-start | bytes 14155780
  44.7 5.1 %copy-start.9 = (f32[512,256]{1,0:T(8,128)S(1)}, f32[512,256]{1,0:T(8,128)}, u32[]{:S(2)}) copy-start(f32[512,256]{1,0:T(8,128)} %param.12) | copy-start | bytes 1572868
  44.8 6.1 %copy-start.22 = (f32[256]{0:T(256)S(1)}, f32[256]{0:T(256)}, u32[]{:S(2)}) copy-start(f32[256]{0:T(256)} %param.13) | copy-start | bytes 3076
  44.8 155.5 %copy-start.8 = (f32[256,256]{1,0:T(8,128)S(1)}, f32[256,256]{1,0:T(8,128)}, u32[]{:S(2)}) copy-start(f32[256,256]{1,0:T(8,128)} %param.10) | copy-start | bytes 786436
  200.2 3.9 %copy-start.5 = (f32[512,256]{1,0:T(8,128)S(1)}, f32[512,256]{1,0:T(8,128)}, u32[]{:S(2)}) copy-start(f32[512,256]{1,0:T(8,128)} %get-tuple-element.14) | copy-start | bytes 1572868
  204.1 20.4 %copy-start.2 = (f32[512,256]{0,1:T(8,128)}, f32[512,256]{0,1:T(8,128)S(1)}, u32[]{:S(2)}) copy-start(f32[512,256]{0,1:T(8,128)S(1)} %get-tuple-element.26) | copy-start | bytes 1572868
  207.2 6.6 %slice-start = ((s8[4718592]{0:T(1024)(128)(4,1)}), s8[4194304]{0:T(1024)(128)(4,1)S(1)}, s32[]{:S(2)}) async-start(s8[4718592]{0:T(1024)(128)(4,1)} %bitcast.46), calls=%async_computation.1 | async-start | bytes 8388608
  208.3 5.5 %slice-start.1 = ((s8[4718592]{0:T(1024)(128)(4,1)}), s8[524288]{0:T(1024)(128)(4,1)S(1)}, s32[]{:S(2)}) async-start(s8[4718592]{0:T(1024)(128)(4,1)} %bitcast.46), calls=%async_computation.2 | async-start | bytes 1048576
  218.1 6.5 %copy-start.6 = (f32[512,256]{0,1:T(8,128)S(1)}, f32[512,256]{0,1:T(8,128)}, u32[]{:S(2)}) copy-start(f32[512,256]{0,1:T(8,128)} %get-tuple-element.15) | copy-start | bytes 1572868
  220.9 6.0 %collective-permute-start.4 = (f32[1,96,256]{2,1,0:T(8,128)S(1)}, f32[1,96,256]{2,1,0:T(8,128)S(1)}, u32[]{:S(2)}, u32[]{:S(2)}) collective-permute-start(f32[1,96,256]{2,1,0:T(8,128)S(1)} %get-tuple-element.22), channel_id=1, source_target_pairs={{0,8},{8,16},{16,24},{24,32},{32,40},{40,48},{48,56},{56,64},{64,7... | collective-permute-start | bytes 294920 | tf_op jit(solution)/shard_map/ppermute | solution.py:15
  223.2 5.4 %collective-permute-start.5 = (f32[1,96,256]{2,1,0:T(8,128)S(1)}, f32[1,96,256]{2,1,0:T(8,128)S(1)}, u32[]{:S(2)}, u32[]{:S(2)}) collective-permute-start(f32[1,96,256]{2,1,0:T(8,128)S(1)} %get-tuple-element.23), channel_id=1, source_target_pairs={{8,0},{16,8},{24,16},{32,24},{40,32},{48,40},{56,48},{64,56},{72,6... | collective-permute-start | bytes 294920 | tf_op jit(solution)/shard_map/ppermute | solution.py:17
  226.9 7.8 %copy-start.7 = (f32[512,256]{1,0:T(8,128)S(1)}, f32[512,256]{1,0:T(8,128)}, u32[]{:S(2)}) copy-start(f32[512,256]{1,0:T(8,128)} %copy.16) | copy-start | bytes 1572868
  226.9 8.6 %copy-start.3 = (f32[512,256]{0,1:T(8,128)S(1)}, f32[512,256]{0,1:T(8,128)}, u32[]{:S(2)}) copy-start(f32[512,256]{0,1:T(8,128)} %copy-done.2) | copy-start | bytes 1572868
  228.6 7.9 %collective-permute-start.6 = (f32[26,1,256]{2,1,0:T(1,128)S(1)}, f32[26,1,256]{2,1,0:T(1,128)S(1)}, u32[]{:S(2)}, u32[]{:S(2)}) collective-permute-start(f32[26,1,256]{2,1,0:T(1,128)S(1)} %get-tuple-element.18), channel_id=1, source_target_pairs={{1,0},{2,1},{3,2},{4,3},{5,4},{6,5},{7,6},{9,8},{10,9},{11,10},{12... | collective-permute-start | bytes 79880 | tf_op jit(solution)/shard_map/ppermute | solution.py:17
  232.7 3.8 %collective-permute-start.7 = (f32[26,1,256]{2,1,0:T(1,128)S(1)}, f32[26,1,256]{2,1,0:T(1,128)S(1)}, u32[]{:S(2)}, u32[]{:S(2)}) collective-permute-start(f32[26,1,256]{2,1,0:T(1,128)S(1)} %get-tuple-element.19), channel_id=1, source_target_pairs={{0,1},{1,2},{2,3},{3,4},{4,5},{5,6},{6,7},{8,9},{9,10},{10,11},{11... | collective-permute-start | bytes 79880 | tf_op jit(solution)/shard_map/ppermute | solution.py:15
  236.5 0.7 copy-start.12
  236.5 0.7 copy-start.14
  236.5 0.7 copy-start.16
  236.5 0.7 copy-start.18
  236.5 0.7 copy-start.20
Sparse Core Ops, SparseCore 0:
  49.9 150.2 all-reduce.2
where the time goes:
time: 250 us; the launch traced here: 248 us
  waiting for transfers between devices  156 us (62%)
  matrix products  31.7 us (13%)
  starting transfers between devices  22.4 us (9%)
  other arithmetic  15.5 us (6%)
  between operations  14.5 us (6%)
  local copies, waits for them, and re-layouts  7.64 us (3%)
    psum x1, waiting for transfers between devices, shards(): by_label, by_grad = lax.psum((by_label, by_grad), ('row', 'col'))  149 us
    dot_general x7, matrix products, matmul(): jnp.dot(left, right, preferred_element_type=jnp.float32, precision=lax.Pr...  18.6 us
    ppermute x4, starting transfers between devices, padded_2(): lax.ppermute(tail, axis, [(i, (i + 1) % count) for i in range(ends)])  13.8 us
    dot_general x4, matrix products, inner_rows(): lax.dot_general(left, right, (((0,), (0,)), ((), ())), preferred_element_...  13.1 us
    add x1, other arithmetic, shards(): mixed = mixed + depth_kernel[a, b] * padded[a:a + rows, b:b + cols]  9.88 us
    ppermute x4, starting transfers between devices, padded_2(): lax.ppermute(head, axis, [((i + 1) % count, i) for i in range(ends)])  8.58 us
    ppermute x4, waiting for transfers between devices, padded_2(): lax.ppermute(head, axis, [((i + 1) % count, i) for i in range(ends)])  6.66 us
    unnamed x54, local copies, waits for them, and re-layouts  5.52 us
  transfers between devices with their start and end apart: 9, of which 5 were waited for; matrix products, arithmetic and copies ran while one was open for 3% of the time, Pallas kernels for 0%

commit v1 on v0

--- a/solution.py
+++ b/solution.py
@@ -1,7 +1,107 @@
 import jax
 import jax.numpy as jnp
 from jax import lax
+from jax.experimental import pallas as pl
+from jax.experimental.pallas import tpu as pltpu
 from jax.sharding import PartitionSpec as P
+
+MESH = pl.DeviceIdType.MESH
+
+
+def place():
+    r, c = lax.axis_index("row"), lax.axis_index("col")
+    return r // 4, lax.rem(r, 4), c // 2, lax.rem(c, 2)
+
+
+def at(x, y, z, k):
+    return (lax.rem(x, 4) * 4 + lax.rem(y, 4), lax.rem(z, 4) * 2 + k)
+
+
+def chip_at(t):
+    x, y, z, k = place()
+    x, y, z = x + t // 16 + 2, y + lax.rem(t // 4, 4) + 2, z + lax.rem(t, 4) + 2
+    x, y, z = lax.rem(x, 4), lax.rem(y, 4), lax.rem(z, 4)
+    return (x * 4 + y, z * 2 + k), x * 16 + y * 4 + z
+
+
+SELF = 42
+
+
+def signal(sem, device):
+    pl.semaphore_signal(sem, inc=1, device_id=device, device_id_type=MESH)
+
+
+def remote(src, dst, send, recv, device):
+    return pltpu.make_async_remote_copy(
+        src_ref=src, dst_ref=dst, send_sem=send, recv_sem=recv, device_id=device, device_id_type=MESH
+    )
+
+
+def others(step):
+    lax.fori_loop(0, SELF, lambda t, _: step(t, t), None)
+    lax.fori_loop(SELF + 1, 64, lambda t, _: step(t, t - 1), None)
+
+
+def all_reduce_kernel(parts, out, partner_part, chip_sum, landing, met, sems):
+    x, y, z, k = place()
+    me = x * 16 + y * 4 + z
+    lines = (
+        [at(x + d, y, z, k) for d in (1, 2, 3)],
+        [at(x, y + d, z, k) for d in (1, 2, 3)],
+        [at(x, y, z + d, k) for d in (1, 2, 3)],
+    )
+    partner = at(x, y, z, 1 - k)
+    barrier = pltpu.get_barrier_semaphore()
+    for device in [*lines[0], *lines[1], *lines[2], partner]:
+        signal(barrier, device)
+    pl.semaphore_wait(barrier, 10)
+    pair = remote(parts.at[1 - k], partner_part, sems.at[0], sems.at[1], partner)
+    pair.start()
+    for stage in range(2):
+        for device in lines[stage]:
+            signal(met.at[stage], device)
+        pl.semaphore_wait(met.at[stage], 3)
+    pair.wait()
+    chip_sum[...] = parts[k] + partner_part[...]
+
+    def scatter(t, slot):
+        device, chip = chip_at(t)
+        remote(chip_sum.at[chip], landing.at[slot], sems.at[2], sems.at[3], device).start()
+
+    others(scatter)
+    pltpu.make_async_copy(landing, landing, sems.at[3]).wait()
+    out[k, me] = chip_sum[me] + jnp.sum(landing[...], axis=0)
+
+    def gather(t, slot):
+        device, _ = chip_at(t)
+        remote(out.at[k, me], out.at[k, me], sems.at[4], sems.at[5], device).start()
+
+    others(gather)
+    pltpu.make_async_copy(landing, landing, sems.at[5]).wait()
+    back = remote(out.at[k], out.at[k], sems.at[6], sems.at[7], partner)
+    back.start()
+    pltpu.make_async_copy(landing, landing, sems.at[2]).wait()
+    pltpu.make_async_copy(landing, landing, sems.at[4]).wait()
+    back.wait()
+
+
+def all_reduce(parts):
+    tile = (64, 8, 256)
+    whole = pl.BlockSpec(memory_space=pltpu.VMEM)
+    return pl.pallas_call(
+        all_reduce_kernel,
+        out_shape=jax.ShapeDtypeStruct((2, *tile), jnp.float32),
+        in_specs=[whole],
+        out_specs=whole,
+        scratch_shapes=[
+            pltpu.VMEM(tile, jnp.float32),
+            pltpu.VMEM(tile, jnp.float32),
+            pltpu.VMEM((63, 8, 256), jnp.float32),
+            pltpu.SemaphoreType.REGULAR((2,)),
+            pltpu.SemaphoreType.DMA((8,)),
+        ],
+        compiler_params=pltpu.CompilerParams(collective_id=0, has_side_effects=True),
+    )(parts)
 
 
 def padded_2(cells, sides, width):
@@ -59,7 +159,9 @@
     grads = cotangent.reshape(-1, count)
     by_label = inner_rows(onehot, mixed)
     by_grad = inner_rows(grads, mixed)
-    by_label, by_grad = lax.psum((by_label, by_grad), ("row", "col"))
+    by_label, by_grad = all_reduce(
+        jnp.stack([by_label, by_grad]).reshape(2, 64, 8, chans)
+    ).reshape(2, count, chans)
     sums = matmul(by_label, value_weight)
     normed, inverse = normalize(sums)
     new_centers = centers + center_gain * normed

time: 250 us -> 120 us (0.48)
  waiting for transfers between devices: 156 us -> 4.47 us
  Pallas kernels: 0 us -> 34.1 us
  between operations: 14.5 us -> 1.08 us
    psum x1 -> x0, waiting for transfers between devices: 149 us -> none  [shards(): by_label, by_grad = lax.psum((by_label, by_grad), ('row', 'col'))]
    pallas_call x0 -> x1, Pallas kernels: none -> 34.1 us  [all_reduce(): pl.pallas_call(all_reduce_kernel, out_shape=jax.ShapeDtypeStruct((2, *til...]
    unnamed x54 -> x50, local copies, waits for them, and re-layouts: 5.52 us -> 5.56 us
  transfers between devices with their start and end apart: 9 -> 8, of which waited for: 5 -> 3; matrix products, arithmetic and copies ran while one was open for 3% -> 8% of each run, Pallas kernels for 0% -> 0%
where the time goes in v1:
time: 120 us; the launch traced here: 119 us
  Pallas kernels  34.1 us (28%)
  matrix products  29.5 us (25%)
  starting transfers between devices  22.1 us (18%)
  other arithmetic  17.5 us (15%)
  local copies, waits for them, and re-layouts  9.78 us (8%)
  waiting for transfers between devices  4.47 us (4%)
    pallas_call x1, Pallas kernels, all_reduce(): pl.pallas_call(all_reduce_kernel, out_shape=jax.ShapeDtypeStruct((2, *til...  34.1 us
    dot_general x7, matrix products, matmul(): jnp.dot(left, right, preferred_element_type=jnp.float32, precision=lax.Pr...  18.6 us
    ppermute x4, starting transfers between devices, padded_2(): lax.ppermute(tail, axis, [(i, (i + 1) % count) for i in range(ends)])  14.4 us
    dot_general x4, matrix products, inner_rows(): lax.dot_general(left, right, (((0,), (0,)), ((), ())), preferred_element_...  10.9 us
    add x1, other arithmetic, shards(): mixed = mixed + depth_kernel[a, b] * padded[a:a + rows, b:b + cols]  10.1 us
    ppermute x4, starting transfers between devices, padded_2(): lax.ppermute(head, axis, [((i + 1) % count, i) for i in range(ends)])  7.69 us
    unnamed x50, local copies, waits for them, and re-layouts  5.56 us
    ppermute x4, waiting for transfers between devices, padded_2(): lax.ppermute(head, axis, [((i + 1) % count, i) for i in range(ends)])  4.46 us
  transfers between devices with their start and end apart: 8, of which 3 were waited for; matrix products, arithmetic and copies ran while one was open for 8% of the time, Pallas kernels for 0%

profile of v1, /device:TPU:1, one launch (start us, length us, event | category | flops | bytes accessed | tf_op | source)
XLA Modules:
  0.0 118.5 jit_solution(9811512275609123089)
XLA Ops:
  0.6 0.0 copy-start
  0.6 1.0 fusion.57
  1.6 4.0 %collective-permute-start = (f32[1,96,256]{2,1,0:T(8,128)S(1)}, f32[1,96,256]{2,1,0:T(8,128)S(1)}, u32[]{:S(2)}, u32[]{:S(2)}) collective-permute-start(f32[1,96,256]{2,1,0:T(8,128)S(1)} %get-tuple-element.23), channel_id=1, source_target_pairs={{0,8},{8,16},{16,24},{24,32},{32,40},{40,48},{48,56},{56,64},{64,7... | collective-permute-start | bytes 294920 | tf_op jit(solution)/shard_map/ppermute | solution.py:115
  5.7 1.3 %collective-permute-start.1 = (f32[1,96,256]{2,1,0:T(8,128)S(1)}, f32[1,96,256]{2,1,0:T(8,128)S(1)}, u32[]{:S(2)}, u32[]{:S(2)}) collective-permute-start(f32[1,96,256]{2,1,0:T(8,128)S(1)} %get-tuple-element.22), channel_id=1, source_target_pairs={{8,0},{16,8},{24,16},{32,24},{40,32},{48,40},{56,48},{64,56},{72,6... | collective-permute-start | bytes 294920 | tf_op jit(solution)/shard_map/ppermute | solution.py:117
  7.0 0.9 fusion.58
  7.9 0.0 copy-start.10
  7.9 0.0 copy-start.12
  7.9 0.0 copy-start.14
  7.9 0.7 broadcast_multiply_fusion.4
  8.6 0.0 collective-permute-done
  8.6 0.0 copy-start.9
  8.6 0.0 copy-start.8
  8.6 1.9 %constant_dynamic-update-slice_fusion.1 = f32[26,96,256]{2,1,0:T(8,128)S(1)} fusion(f32[26,96,256]{2,1,0:T(8,128)S(1)} %constant_dynamic-update-slice_fusion.2, f32[24,96,256]{2,1,0:T(8,128)} %param.8), kind=kLoop, calls=%fused_computation.95 | loop fusion | bytes 4718592
  10.5 0.5 collective-permute-done.1
  11.1 0.0 copy-start.5
  11.1 1.5 %copy-done.5 = f32[26,96,256]{2,1,0:T(8,128)} copy-done((f32[26,96,256]{2,1,0:T(8,128)}, f32[26,96,256]{2,1,0:T(8,128)S(1)}, u32[]{:S(2)}) %copy-start.5) | copy-done | bytes 2555928
  12.6 5.5 %collective-permute-start.2 = (f32[26,1,256]{2,1,0:T(1,128)S(1)}, f32[26,1,256]{2,1,0:T(1,128)S(1)}, u32[]{:S(2)}, u32[]{:S(2)}) collective-permute-start(f32[26,1,256]{2,1,0:T(1,128)S(1)} %get-tuple-element.18), channel_id=1, source_target_pairs={{0,1},{1,2},{2,3},{3,4},{4,5},{5,6},{6,7},{8,9},{9,10},{10,11},{11... | collective-permute-start | bytes 79880 | tf_op jit(solution)/shard_map/ppermute | solution.py:115
  18.1 1.9 %collective-permute-start.3 = (f32[26,1,256]{2,1,0:T(1,128)S(1)}, f32[26,1,256]{2,1,0:T(1,128)S(1)}, u32[]{:S(2)}, u32[]{:S(2)}) collective-permute-start(f32[26,1,256]{2,1,0:T(1,128)S(1)} %get-tuple-element.19), channel_id=1, source_target_pairs={{1,0},{2,1},{3,2},{4,3},{5,4},{6,5},{7,6},{9,8},{10,9},{11,10},{12... | collective-permute-start | bytes 79880 | tf_op jit(solution)/shard_map/ppermute | solution.py:117
  20.1 0.1 eq.37
  20.1 0.0 copy-done.8
  20.2 1.0 copy.15
  21.1 0.0 collective-permute-done.2
  21.2 2.1 %collective-permute-done.3 = f32[26,1,256]{2,1,0:T(1,128)S(1)} collective-permute-done((f32[26,1,256]{2,1,0:T(1,128)S(1)}, f32[26,1,256]{2,1,0:T(1,128)S(1)}, u32[]{:S(2)}, u32[]{:S(2)}) %collective-permute-start.3) | collective-permute-done | bytes 26656 | tf_op jit(solution)/shard_map/ppermute | solution.py:117
  23.3 0.0 copy-start.1
  23.3 10.1 %fusion.9 = f32[24,96,256]{2,1,0:T(8,128)S(1)} fusion(f32[26,96,256]{2,1,0:T(8,128)} %copy-done.5, f32[24,96,256]{2,1,0:T(8,128)} %param.8, f32[26,1,256]{2,1,0:T(1,128)S(1)} %collective-permute-done.3, f32[26,1,256]{2,1,0:T(1,128)S(1)} %collective-permute-done.2, f32[1,96,256]{2,1,0:T(8,128)S(1)} %collective-permute-done.1, ...), kind=kLoop, calls=%fused_computation.21 | loop fusion | flops 15335424 | bytes 7533568 | tf_op jit(solution)/shard_map/add | solution.py:154
  33.5 4.9 %convolution_bitcast_fusion.1 = f32[512,256]{0,1:T(8,128)} fusion(f32[24,96,256]{2,1,0:T(8,128)S(1)} %fusion.9, f32[24,96,512]{2,1,0:T(8,128)S(1)} %copy-done.1), kind=kOutput, calls=%fused_computation.64 | convolution fusion | flops 3623878656 | bytes 7602176 | tf_op jit(solution)/shard_map/dot_general | solution.py:129
  38.4 1.2 %copy.14 = f32[512,256]{1,0:T(8,128)S(1)} copy(f32[512,256]{0,1:T(8,128)} %convolution_bitcast_fusion.1) | data formatting | bytes 1048576 | tf_op jit(solution)/shard_map/dot_general | solution.py:129
  39.7 2.4 %fusion.39 = f32[1,64,8,256]{3,2,1,0:T(8,128)S(1)} fusion(f32[2304,256,1]{1,0,2:T(8,128)S(1)} %bitcast.60, s32[64,8]{1,0:T(8,128)S(1)} %multiply_add_fusion.1, s32[2304]{0:T(1024)S(1)} %eq.37), kind=kOutput, calls=%fused_computation.63 | convolution fusion | flops 3625058304 | bytes 2894848 | tf_op jit(solution)/shard_map/dot_general | solution.py:129
  42.1 0.0 copy-start.7
  42.1 1.0 pad_maximum_fusion.7.parts
  43.1 34.1 %shard_map.127 = f32[2,64,8,256]{3,2,1,0:T(8,128)} custom-call(f32[2,64,8,256]{3,2,1,0:T(8,128)} %pad_maximum_fusion.7.parts), custom_call_target="tpu_custom_call" | custom-call | tf_op jit(solution)/shard_map/pallas_call | solution.py:91
  77.2 0.0 copy-done.7
  77.2 0.0 copy-start.2
  77.2 1.8 %fusion.59 = (f32[512]{0:T(512)S(1)}, f32[512,256]{0,1:T(8,128)S(1)}) fusion(f32[256,256]{1,0:T(8,128)S(1)} %copy-done.7, f32[2,64,8,256]{3,2,1,0:T(8,128)} %shard_map.127), kind=kOutput, calls=%fused_computation.106 | convolution fusion | flops 402783744 | bytes 1312768 | tf_op jit(solution)/shard_map/dot_general | solution.py:125
  79.0 0.1 multiply_reduce_fusion.1
  79.1 0.0 copy-done
  79.1 0.0 copy-done.20
  79.1 2.0 %multiply_reduce_fusion.2 = (f32[512]{0:T(512)S(1)}, f32[512]{0:T(512)S(1)}, f32[512,256]{0,1:T(8,128)S(1)}, f32[512,256]{0,1:T(8,128)S(1)}) fusion(f32[256]{0:T(256)S(1)} %broadcast_multiply_fusion.4, f32[512]{0:T(512)S(1)} %add_rsqrt_fusion, f32[512,256]{0,1:T(8,128)S(1)} %get-tuple-element.35, f32[512]{0:T(512)S(1)} %broadcast_multiply_fusion.3, ...), kind=kOutput, calls=%fused_computation.86 | convolution fusion | flops 403700736 | bytes 2893824 | tf_op jit(solution)/shard_map/dot_general | solution.py:125
  81.1 0.0 copy-start.3
  81.2 1.8 %fusion.47 = f32[256,256]{1,0:T(8,128)} fusion(f32[2,64,8,256]{3,2,1,0:T(8,128)S(1)} %copy-done.2, f32[512,256]{0,1:T(8,128)S(1)} %get-tuple-element.36, f32[512,256]{0,1:T(8,128)S(1)} %get-tuple-element.35, f32[512]{0:T(512)S(1)} %get-tuple-element.37, f32[512]{0:T(512)S(1)} %get-tuple-element.38, f32[256]{0:T(256)S(1)} %broadcast_multiply_fusion.4, ...), kind=kOutput, calls=%fused_computation.73 | convolution fusion | flops 403570688 | bytes 1844224 | tf_op jit(solution)/shard_map/dot_general | solution.py:129
  83.0 1.1 fusion.55
  84.1 0.0 slice-start
  84.1 1.0 convolution_multiply_fusion
  85.1 0.0 slice-start.1
  85.1 5.5 %fusion.45 = f32[24,96,512]{2,1,0:T(8,128)} fusion(f32[24,96,256]{2,1,0:T(8,128)S(1)} %fusion.9, f32[512,256]{1,0:T(8,128)S(1)} %convolution_multiply_fusion), kind=kOutput, calls=%fused_computation.71 | convolution fusion | flops 3623878656 | bytes 7602176 | tf_op jit(solution)/shard_map/dot_general | solution.py:125
  90.7 4.3 %convolution_bitcast_fusion = f32[2304,256]{1,0:T(8,128)S(1)} fusion(f32[512,256]{1,0:T(8,128)S(1)} %convolution_multiply_fusion, f32[2304,512]{1,0:T(8,128)S(1)} %bitcast.63), kind=kOutput, calls=%fused_computation.5 | convolution fusion | flops 3623878656 | bytes 7602176 | tf_op jit(solution)/shard_map/dot_general | solution.py:125
  94.9 3.0 %fusion.3 = f32[2304,256]{1,0:T(8,128)S(1)} fusion(f32[2304,256]{1,0:T(8,128)S(1)} %convolution_bitcast_fusion, f32[512,256]{1,0:T(8,128)S(1)} %fusion.55, s32[2304]{0:T(1024)S(1)} %eq.37), kind=kOutput, calls=%fused_computation.4 | convolution fusion | flops 3625648128 | bytes 5252096 | tf_op jit(solution)/shard_map/dot_general | solution.py:125
  97.9 2.2 %collective-permute-start.4 = (f32[1,96,256]{2,1,0:T(8,128)S(1)}, f32[1,96,256]{2,1,0:T(8,128)S(1)}, u32[]{:S(2)}, u32[]{:S(2)}) collective-permute-start(f32[1,96,256]{2,1,0:T(8,128)S(1)} %get-tuple-element.20), channel_id=1, source_target_pairs={{0,8},{8,16},{16,24},{24,32},{32,40},{40,48},{48,56},{56,64},{64,7... | collective-permute-start | bytes 294920 | tf_op jit(solution)/shard_map/ppermute | solution.py:115
  100.2 1.3 %collective-permute-start.5 = (f32[1,96,256]{2,1,0:T(8,128)S(1)}, f32[1,96,256]{2,1,0:T(8,128)S(1)}, u32[]{:S(2)}, u32[]{:S(2)}) collective-permute-start(f32[1,96,256]{2,1,0:T(8,128)S(1)} %get-tuple-element.21), channel_id=1, source_target_pairs={{8,0},{16,8},{24,16},{32,24},{40,32},{48,40},{56,48},{64,56},{72,6... | collective-permute-start | bytes 294920 | tf_op jit(solution)/shard_map/ppermute | solution.py:117
  101.5 0.0 copy-done.3
  101.5 1.7 %convolution_multiply_fusion.1 = f32[256,256]{1,0:T(8,128)} fusion(f32[512,256]{0,1:T(8,128)S(1)} %get-tuple-element.24, f32[2,64,8,256]{3,2,1,0:T(8,128)S(1)} %copy-done.2), kind=kOutput, calls=%fused_computation.66 | convolution fusion | flops 402718720 | bytes 1310720 | tf_op jit(solution)/shard_map/dot_general | solution.py:129
  103.2 1.0 copy.17
  104.2 0.0 collective-permute-done.4
  104.2 1.8 %collective-permute-done.5 = f32[1,96,256]{2,1,0:T(8,128)S(1)} collective-permute-done((f32[1,96,256]{2,1,0:T(8,128)S(1)}, f32[1,96,256]{2,1,0:T(8,128)S(1)}, u32[]{:S(2)}, u32[]{:S(2)}) %collective-permute-start.5) | collective-permute-done | bytes 98336 | tf_op jit(solution)/shard_map/ppermute | solution.py:117
  106.0 3.2 %collective-permute-start.6 = (f32[26,1,256]{2,1,0:T(1,128)S(1)}, f32[26,1,256]{2,1,0:T(1,128)S(1)}, u32[]{:S(2)}, u32[]{:S(2)}) collective-permute-start(f32[26,1,256]{2,1,0:T(1,128)S(1)} %get-tuple-element.16), channel_id=1, source_target_pairs={{1,0},{2,1},{3,2},{4,3},{5,4},{6,5},{7,6},{9,8},{10,9},{11,10},{12... | collective-permute-start | bytes 79880 | tf_op jit(solution)/shard_map/ppermute | solution.py:117
  109.2 2.6 %collective-permute-start.7 = (f32[26,1,256]{2,1,0:T(1,128)S(1)}, f32[26,1,256]{2,1,0:T(1,128)S(1)}, u32[]{:S(2)}, u32[]{:S(2)}) collective-permute-start(f32[26,1,256]{2,1,0:T(1,128)S(1)} %get-tuple-element.17), channel_id=1, source_target_pairs={{0,1},{1,2},{2,3},{3,4},{4,5},{5,6},{6,7},{8,9},{9,10},{10,11},{11... | collective-permute-start | bytes 79880 | tf_op jit(solution)/shard_map/ppermute | solution.py:115
  111.9 0.8 broadcast_multiply_fusion
  112.7 1.0 copy.18
  113.7 0.0 collective-permute-done.6
  113.7 0.0 collective-permute-done.7
  113.8 0.5 pad_maximum_fusion
  114.3 0.1 copy-done.11
  114.4 0.0 copy-done.19
  114.4 4.1 %fusion.21 = f32[24,96,256]{2,1,0:T(8,128)} fusion(f32[26,97,256]{2,1,0:T(8,128)S(1)} %get-tuple-element.15, f32[24,96,256]{2,1,0:T(8,128)S(1)} %bitcast.59, f32[1,96,256]{2,1,0:T(8,128)S(1)} %collective-permute-done.4, f32[26,97,256]{2,1,0:T(8,128)S(1)} %get-tuple-element.14, f32[1,96,256]{2,1,0:T(8,128)S(1)} %collective-permute-done.5, ...), kind=kLoop, calls=%fused_computation.34 | loop fusion | flops 11796480 | bytes 19080192 | tf_op jit(solution)/shard_map/add | solution.py:187
  (35 shorter events, 0.2 us)
Async XLA Ops:
  0.6 78.5 %copy-start = (f32[256,256]{1,0:T(8,128)S(1)}, f32[256,256]{1,0:T(8,128)}, u32[]{:S(2)}) copy-start(f32[256,256]{1,0:T(8,128)} %param.11) | copy-start | bytes 786436
  1.6 6.9 %collective-permute-start = (f32[1,96,256]{2,1,0:T(8,128)S(1)}, f32[1,96,256]{2,1,0:T(8,128)S(1)}, u32[]{:S(2)}, u32[]{:S(2)}) collective-permute-start(f32[1,96,256]{2,1,0:T(8,128)S(1)} %get-tuple-element.23), channel_id=1, source_target_pairs={{0,8},{8,16},{16,24},{24,32},{32,40},{40,48},{48,56},{56,64},{64,7... | collective-permute-start | bytes 294920 | tf_op jit(solution)/shard_map/ppermute | solution.py:115
  5.7 5.4 %collective-permute-start.1 = (f32[1,96,256]{2,1,0:T(8,128)S(1)}, f32[1,96,256]{2,1,0:T(8,128)S(1)}, u32[]{:S(2)}, u32[]{:S(2)}) collective-permute-start(f32[1,96,256]{2,1,0:T(8,128)S(1)} %get-tuple-element.22), channel_id=1, source_target_pairs={{8,0},{16,8},{24,16},{32,24},{40,32},{48,40},{56,48},{64,56},{72,6... | collective-permute-start | bytes 294920 | tf_op jit(solution)/shard_map/ppermute | solution.py:117
  7.9 15.4 %copy-start.10 = (f32[1,1,256]{2,1,0:T(1,128)}, f32[1,1,256]{2,1,0:T(1,128)S(1)}, u32[]{:S(2)}) copy-start(f32[1,1,256]{2,1,0:T(1,128)S(1)} %get-tuple-element.29) | copy-start | bytes 3076
  7.9 15.4 %copy-start.12 = (f32[1,1,256]{2,1,0:T(1,128)}, f32[1,1,256]{2,1,0:T(1,128)S(1)}, u32[]{:S(2)}) copy-start(f32[1,1,256]{2,1,0:T(1,128)S(1)} %get-tuple-element.30) | copy-start | bytes 3076
  7.9 15.4 %copy-start.14 = (f32[1,1,256]{2,1,0:T(1,128)}, f32[1,1,256]{2,1,0:T(1,128)S(1)}, u32[]{:S(2)}) copy-start(f32[1,1,256]{2,1,0:T(1,128)S(1)} %get-tuple-element.31) | copy-start | bytes 3076
  7.9 15.4 %copy-start.16 = (f32[1,1,256]{2,1,0:T(1,128)}, f32[1,1,256]{2,1,0:T(1,128)S(1)}, u32[]{:S(2)}) copy-start(f32[1,1,256]{2,1,0:T(1,128)S(1)} %get-tuple-element.32) | copy-start | bytes 3076
  7.9 15.4 %copy-start.18 = (f32[1,1,256]{2,1,0:T(1,128)}, f32[1,1,256]{2,1,0:T(1,128)S(1)}, u32[]{:S(2)}) copy-start(f32[1,1,256]{2,1,0:T(1,128)S(1)} %get-tuple-element.33) | copy-start | bytes 3076
  8.6 11.5 %copy-start.9 = (s32[24,96]{1,0:T(8,128)S(1)}, s32[24,96]{1,0:T(8,128)}, u32[]{:S(2)}) copy-start(s32[24,96]{1,0:T(8,128)} %param.14) | copy-start | bytes 27652
  8.6 11.5 %copy-start.8 = (f32[512,256]{1,0:T(8,128)S(1)}, f32[512,256]{1,0:T(8,128)}, u32[]{:S(2)}) copy-start(f32[512,256]{1,0:T(8,128)} %param.12) | copy-start | bytes 1572868
  11.1 1.5 %copy-start.5 = (f32[26,96,256]{2,1,0:T(8,128)}, f32[26,96,256]{2,1,0:T(8,128)S(1)}, u32[]{:S(2)}) copy-start(f32[26,96,256]{2,1,0:T(8,128)S(1)} %constant_dynamic-update-slice_fusion) | copy-start | bytes 7667716
  12.6 8.6 %collective-permute-start.2 = (f32[26,1,256]{2,1,0:T(1,128)S(1)}, f32[26,1,256]{2,1,0:T(1,128)S(1)}, u32[]{:S(2)}, u32[]{:S(2)}) collective-permute-start(f32[26,1,256]{2,1,0:T(1,128)S(1)} %get-tuple-element.18), channel_id=1, source_target_pairs={{0,1},{1,2},{2,3},{3,4},{4,5},{5,6},{6,7},{8,9},{9,10},{10,11},{11... | collective-permute-start | bytes 79880 | tf_op jit(solution)/shard_map/ppermute | solution.py:115
  18.1 5.2 %collective-permute-start.3 = (f32[26,1,256]{2,1,0:T(1,128)S(1)}, f32[26,1,256]{2,1,0:T(1,128)S(1)}, u32[]{:S(2)}, u32[]{:S(2)}) collective-permute-start(f32[26,1,256]{2,1,0:T(1,128)S(1)} %get-tuple-element.19), channel_id=1, source_target_pairs={{1,0},{2,1},{3,2},{4,3},{5,4},{6,5},{7,6},{9,8},{10,9},{11,10},{12... | collective-permute-start | bytes 79880 | tf_op jit(solution)/shard_map/ppermute | solution.py:117
  23.3 10.1 %copy-start.1 = (f32[24,96,512]{2,1,0:T(8,128)S(1)}, f32[24,96,512]{2,1,0:T(8,128)}, u32[]{:S(2)}) copy-start(f32[24,96,512]{2,1,0:T(8,128)} %param.15) | copy-start | bytes 14155780
  42.1 35.1 %copy-start.7 = (f32[256,256]{1,0:T(8,128)S(1)}, f32[256,256]{1,0:T(8,128)}, u32[]{:S(2)}) copy-start(f32[256,256]{1,0:T(8,128)} %param.10) | copy-start | bytes 786436
  43.1 36.0 %copy-start.20 = (f32[256]{0:T(256)S(1)}, f32[256]{0:T(256)}, u32[]{:S(2)}) copy-start(f32[256]{0:T(256)} %param.13) | copy-start | bytes 3076
  77.2 3.9 %copy-start.2 = (f32[2,64,8,256]{3,2,1,0:T(8,128)S(1)}, f32[2,64,8,256]{3,2,1,0:T(8,128)}, u32[]{:S(2)}) copy-start(f32[2,64,8,256]{3,2,1,0:T(8,128)} %shard_map.127) | copy-start | bytes 3145732
  81.1 20.4 %copy-start.3 = (f32[512,256]{0,1:T(8,128)}, f32[512,256]{0,1:T(8,128)S(1)}, u32[]{:S(2)}) copy-start(f32[512,256]{0,1:T(8,128)S(1)} %get-tuple-element.24) | copy-start | bytes 1572868
  84.1 6.6 %slice-start = ((s8[4718592]{0:T(1024)(128)(4,1)}), s8[4194304]{0:T(1024)(128)(4,1)S(1)}, s32[]{:S(2)}) async-start(s8[4718592]{0:T(1024)(128)(4,1)} %bitcast.61), calls=%async_computation | async-start | bytes 8388608
  85.1 5.5 %slice-start.1 = ((s8[4718592]{0:T(1024)(128)(4,1)}), s8[524288]{0:T(1024)(128)(4,1)S(1)}, s32[]{:S(2)}) async-start(s8[4718592]{0:T(1024)(128)(4,1)} %bitcast.61), calls=%async_computation.1 | async-start | bytes 1048576
  97.9 6.3 %collective-permute-start.4 = (f32[1,96,256]{2,1,0:T(8,128)S(1)}, f32[1,96,256]{2,1,0:T(8,128)S(1)}, u32[]{:S(2)}, u32[]{:S(2)}) collective-permute-start(f32[1,96,256]{2,1,0:T(8,128)S(1)} %get-tuple-element.20), channel_id=1, source_target_pairs={{0,8},{8,16},{16,24},{24,32},{32,40},{40,48},{48,56},{56,64},{64,7... | collective-permute-start | bytes 294920 | tf_op jit(solution)/shard_map/ppermute | solution.py:115
  100.2 5.8 %collective-permute-start.5 = (f32[1,96,256]{2,1,0:T(8,128)S(1)}, f32[1,96,256]{2,1,0:T(8,128)S(1)}, u32[]{:S(2)}, u32[]{:S(2)}) collective-permute-start(f32[1,96,256]{2,1,0:T(8,128)S(1)} %get-tuple-element.21), channel_id=1, source_target_pairs={{8,0},{16,8},{24,16},{32,24},{40,32},{48,40},{56,48},{64,56},{72,6... | collective-permute-start | bytes 294920 | tf_op jit(solution)/shard_map/ppermute | solution.py:117
  104.2 7.7 %copy-start.6 = (f32[512,256]{1,0:T(8,128)S(1)}, f32[512,256]{1,0:T(8,128)}, u32[]{:S(2)}) copy-start(f32[512,256]{1,0:T(8,128)} %copy.17) | copy-start | bytes 1572868
  104.2 8.5 %copy-start.4 = (f32[512,256]{0,1:T(8,128)S(1)}, f32[512,256]{0,1:T(8,128)}, u32[]{:S(2)}) copy-start(f32[512,256]{0,1:T(8,128)} %copy-done.3) | copy-start | bytes 1572868
  106.0 7.7 %collective-permute-start.6 = (f32[26,1,256]{2,1,0:T(1,128)S(1)}, f32[26,1,256]{2,1,0:T(1,128)S(1)}, u32[]{:S(2)}, u32[]{:S(2)}) collective-permute-start(f32[26,1,256]{2,1,0:T(1,128)S(1)} %get-tuple-element.16), channel_id=1, source_target_pairs={{1,0},{2,1},{3,2},{4,3},{5,4},{6,5},{7,6},{9,8},{10,9},{11,10},{12... | collective-permute-start | bytes 79880 | tf_op jit(solution)/shard_map/ppermute | solution.py:117
  109.2 4.5 %collective-permute-start.7 = (f32[26,1,256]{2,1,0:T(1,128)S(1)}, f32[26,1,256]{2,1,0:T(1,128)S(1)}, u32[]{:S(2)}, u32[]{:S(2)}) collective-permute-start(f32[26,1,256]{2,1,0:T(1,128)S(1)} %get-tuple-element.17), channel_id=1, source_target_pairs={{0,1},{1,2},{2,3},{3,4},{4,5},{5,6},{6,7},{8,9},{9,10},{10,11},{11... | collective-permute-start | bytes 79880 | tf_op jit(solution)/shard_map/ppermute | solution.py:115
  113.7 0.7 copy-start.11
  113.7 0.7 copy-start.13
  113.7 0.7 copy-start.15
  113.7 0.7 copy-start.17
  113.7 0.7 copy-start.19

commit v2 on v1

v2 whole, which is shorter than its diff:
```python
import jax
import jax.numpy as jnp
from jax import lax
from jax.experimental import pallas as pl
from jax.experimental.pallas import tpu as pltpu
from jax.sharding import PartitionSpec as P

MESH = pl.DeviceIdType.MESH
HIGH = lax.Precision.HIGH
ROWS, COLS, CHANS, COUNT = 24, 96, 256, 512
GRID_ROWS, GRID_COLS = 16, 8
CELLS = ROWS * COLS
STRIP = 48
NORTH, SOUTH, WEST, EAST = CELLS, CELLS + COLS, CELLS + 2 * COLS, CELLS + 2 * COLS + STRIP
FULL = CELLS + 2 * COLS + 2 * STRIP
SCALE = 1.0 / 16.0
SELF = 42
TILE = (64, 8, 256)
SIDES = ((-1, 0), (1, 0), (0, -1), (0, 1), (-1, -1), (-1, 1), (1, -1), (1, 1))
OPPOSITE = (1, 0, 3, 2, 7, 6, 5, 4)
WHOLE = pl.BlockSpec(memory_space=pltpu.VMEM)
OUTSIDE = pl.BlockSpec(memory_space=pltpu.HBM)


def place():
    r, c = lax.axis_index("row"), lax.axis_index("col")
    return r // 4, lax.rem(r, 4), c // 2, lax.rem(c, 2)


def at(x, y, z, k):
    return (lax.rem(x, 4) * 4 + lax.rem(y, 4), lax.rem(z, 4) * 2 + k)


def chip_at(t):
    x, y, z, k = place()
    x, y, z = x + t // 16 + 2, y + lax.rem(t // 4, 4) + 2, z + lax.rem(t, 4) + 2
    x, y, z = lax.rem(x, 4), lax.rem(y, 4), lax.rem(z, 4)
    return (x * 4 + y, z * 2 + k), x * 16 + y * 4 + z


def signal(sem, device):
    pl.semaphore_signal(sem, inc=1, device_id=device, device_id_type=MESH)


def remote(src, dst, send, recv, device):
    return pltpu.make_async_remote_copy(
        src_ref=src, dst_ref=dst, send_sem=send, recv_sem=recv, device_id=device, device_id_type=MESH
    )


def others(step):
    lax.fori_loop(0, SELF, lambda t, _: step(t, t), None)
    lax.fori_loop(SELF + 1, 64, lambda t, _: step(t, t - 1), None)


def halves(value):
    high = value.astype(jnp.bfloat16)
    return high, (value - high.astype(jnp.float32)).astype(jnp.bfloat16)


def product(left, right, dims=((1,), (0,))):
    return lax.dot_general(left, right, (dims, ((), ())), preferred_element_type=jnp.float32)


def precise(left, right, dims=((1,), (0,))):
    return lax.dot_general(
        left, right, (dims, ((), ())), preferred_element_type=jnp.float32, precision=HIGH
    )


def later(value, edge=None):
    moved = pltpu.roll(value, 1, 0)
    first = lax.broadcasted_iota(jnp.int32, value.shape, 0) == 0
    return jnp.where(first, 0.0 if edge is None else edge, moved)


def earlier(value, edge=None):
    moved = pltpu.roll(value, value.shape[0] - 1, 0)
    last = lax.broadcasted_iota(jnp.int32, value.shape, 0) == value.shape[0] - 1
    return jnp.where(last, 0.0 if edge is None else edge, moved)


def onehot(column, rows):
    clusters = lax.broadcasted_iota(jnp.int32, (rows, COUNT), 1).astype(jnp.float32)
    return jnp.where(column == clusters, 1.0, 0.0).astype(jnp.bfloat16)


def strip_sum(strip, taps):
    return (
        taps[0] * strip[7 : 7 + ROWS, :]
        + taps[1] * strip[8 : 8 + ROWS, :]
        + taps[2] * strip[9 : 9 + ROWS, :]
    )


def halo_copies(own, rows, strips, ends, corners, send, recv, first):
    targets = (
        (own.at[first], rows.at[1]),
        (own.at[first + ROWS - 1], rows.at[0]),
        (ends.at[0], strips.at[1, pl.ds(8, ROWS)]),
        (ends.at[1], strips.at[0, pl.ds(8, ROWS)]),
        (corners.at[0], strips.at[1, pl.ds(32, 8)]),
        (corners.at[1], strips.at[0, pl.ds(32, 8)]),
        (corners.at[2], strips.at[1, pl.ds(0, 8)]),
        (corners.at[3], strips.at[0, pl.ds(0, 8)]),
    )
    return [
        remote(src, dst, send.at[i], recv.at[i], beside(*SIDES[i]))
        for i, (src, dst) in enumerate(targets)
    ]


def beside(dr, dc):
    r, c = lax.axis_index("row"), lax.axis_index("col")
    return (lax.rem(r + dr + GRID_ROWS, GRID_ROWS), lax.rem(c + dc + GRID_COLS, GRID_COLS))


def pack(own, ends, corners, first):
    for i in range(ROWS):
        ends[0, i : i + 1, :] = own[first + i, 0:1, :]
        ends[1, i : i + 1, :] = own[first + i, COLS - 1 : COLS, :]
    for n, (i, j) in enumerate(((0, 0), (0, COLS - 1), (ROWS - 1, 0), (ROWS - 1, COLS - 1))):
        corners[n] = jnp.broadcast_to(own[first + i, j : j + 1, :], corners.shape[1:])


def clear_outside(rows, strips):
    r, c = lax.axis_index("row"), lax.axis_index("col")

    @pl.when(r == 0)
    def _():
        rows[0] = jnp.zeros_like(rows[0])
        for side in range(2):
            strips[side, 0:8, :] = jnp.zeros_like(strips[side, 0:8, :])

    @pl.when(r == GRID_ROWS - 1)
    def _():
        rows[1] = jnp.zeros_like(rows[1])
        for side in range(2):
            strips[side, 32:40, :] = jnp.zeros_like(strips[side, 32:40, :])

    for side, edge in ((0, 0), (1, GRID_COLS - 1)):

        @pl.when(c == edge)
        def _():
            strips[side] = jnp.zeros_like(strips[side])


def reduce_kernel(
    features,
    cotangent,
    labels,
    taps_in,
    sums,
    mixed_pair,
    grads_high,
    grads_low,
    ones,
    fx,
    gx,
    lab,
    taps,
    fn,
    gn,
    fs,
    gs,
    f_ends,
    g_ends,
    f_corners,
    g_corners,
    lab_near,
    lab_square,
    mixed,
    mixed_t,
    rim_t,
    rim_ones,
    rim_high,
    rim_low,
    totals,
    parts,
    partner_part,
    chip_sum,
    landing,
    load,
    met,
    sems,
    f_send,
    f_recv,
    g_send,
    g_recv,
    l_send,
    l_recv,
):
    r, c = lax.axis_index("row"), lax.axis_index("col")
    x, y, z, k = place()
    me = x * 16 + y * 4 + z
    lines = (
        [at(x + d, y, z, k) for d in (1, 2, 3)],
        [at(x, y + d, z, k) for d in (1, 2, 3)],
        [at(x, y, z + d, k) for d in (1, 2, 3)],
    )
    partner = at(x, y, z, 1 - k)
    load_labels = pltpu.make_async_copy(labels, lab, load.at[0])
    load_taps = pltpu.make_async_copy(taps_in, taps, load.at[1])
    load_labels.start()
    load_taps.start()
    load_f = [
        pltpu.make_async_copy(
            features.at[pl.ds(8 * n, 8)], fx.at[pl.ds(1 + 8 * n, 8)], load.at[2 + n]
        )
        for n in range(3)
    ]
    load_g = [
        pltpu.make_async_copy(cotangent.at[pl.ds(8 * n, 8)], gx.at[pl.ds(8 * n, 8)], load.at[5 + n])
        for n in range(3)
    ]
    for copy in (*load_f, *load_g):
        copy.start()
    barrier = pltpu.get_barrier_semaphore()
    for device in [*lines[0], *lines[1], *lines[2], partner, *(beside(*side) for side in SIDES)]:
        signal(barrier, device)

    fx[0] = jnp.zeros_like(fx[0])
    fx[1 + ROWS] = jnp.zeros_like(fx[0])
    load_labels.wait()
    load_taps.wait()
    lab_square[0:ROWS, 0:COLS] = lab[...].astype(jnp.float32)
    by_column = lab_square[...].T
    for i in range(ROWS):
        ones[COLS * i : COLS * (i + 1), :] = onehot(by_column[0:COLS, i : i + 1], COLS)
    for copy in load_f:
        copy.wait()
    pack(fx, f_ends, f_corners, 1)
    for copy in load_g:
        copy.wait()
    pack(gx, g_ends, g_corners, 0)
    pl.semaphore_wait(barrier, 10 + len(SIDES))
    f_copies = halo_copies(fx, fn, fs, f_ends, f_corners, f_send, f_recv, 1)
    g_copies = halo_copies(gx, gn, gs, g_ends, g_corners, g_send, g_recv, 0)
    l_copies = [
        remote(lab, lab_near.at[OPPOSITE[i]], l_send.at[i], l_recv.at[i], beside(*side))
        for i, side in enumerate(SIDES)
    ]
    for copy in f_copies:
        copy.start()
    for device in lines[0]:
        signal(met.at[0], device)
    for copy in (*g_copies, *l_copies):
        copy.start()

    tap = [taps[n // 3, n % 3 : n % 3 + 1] for n in range(9)]

    def mix(i, _):
        above, here, below = fx[i], fx[i + 1], fx[i + 2]
        t = [
            tap[b] * above + tap[3 + b] * here + tap[6 + b] * below for b in range(3)
        ]
        mixed[i] = here + t[1] + later(t[0]) + earlier(t[2])
        cell = pl.ds(pl.multiple_of(i * COLS, COLS), COLS)
        grads_high[cell, :], grads_low[cell, :] = halves(gx[i])

    lax.fori_loop(0, ROWS, mix, None)
    for n in range(9):
        block = mixed[...].reshape(CELLS, CHANS)[256 * n : 256 * (n + 1)].T
        mixed_t[0:256, 256 * n : 256 * (n + 1)], mixed_t[256:512, 256 * n : 256 * (n + 1)] = halves(
            block
        )
    pl.semaphore_wait(met.at[0], 3)
    for device in lines[1]:
        signal(met.at[1], device)
    by_label = product(mixed_t[...], ones[0:CELLS, :])
    totals[0] = by_label[0:256] + by_label[256:512]
    by_grad = product(mixed_t[...], grads_high[0:CELLS, :])
    totals[1] = (
        by_grad[0:256] + by_grad[256:512] + product(mixed_t[0:256, :], grads_low[0:CELLS, :])
    )

    rim_ones[...] = jnp.zeros_like(rim_ones)
    rim_high[...] = jnp.zeros_like(rim_high)
    rim_low[...] = jnp.zeros_like(rim_low)
    for rim, own in ((rim_ones, ones), (rim_high, grads_high), (rim_low, grads_low)):
        rim[0:COLS, :] = own[0:COLS, :]
        rim[COLS : 2 * COLS, :] = own[CELLS - COLS : CELLS, :]
    fill = jnp.zeros((8, COUNT), jnp.float32)
    for side, column in ((0, 0), (1, COLS - 1)):
        cell = slice(192 + 32 * side, 224 + 32 * side)
        rim_high[cell, :], rim_low[cell, :] = halves(
            jnp.concatenate([g_ends[side], fill], axis=0)
        )
        rim_ones[cell, :] = onehot(lab_square[0:32, column : column + 1], 32)

    for copy in f_copies:
        copy.wait_recv()
    clear_outside(fn, fs)
    north = tap[1] * fn[0] + later(tap[0] * fn[0]) + earlier(tap[2] * fn[0])
    south = tap[7] * fn[1] + later(tap[6] * fn[1]) + earlier(tap[8] * fn[1])
    west = strip_sum(fs.at[0], [tap[3 * a] for a in range(3)])
    east = strip_sum(fs.at[1], [tap[3 * a + 2] for a in range(3)])
    gap = jnp.zeros((8, CHANS), jnp.float32)
    rim = jnp.concatenate([north, south, west, gap, east, gap], axis=0)
    rim_t[0:256, :], rim_t[256:512, :] = halves(rim.T)
    by_label = product(rim_t[...], rim_ones[...])
    parts[0] = (totals[0] + by_label[0:256] + by_label[256:512]).T.reshape(TILE)
    by_grad = product(rim_t[...], rim_high[...])
    by_grad = by_grad[0:256] + by_grad[256:512] + product(rim_t[0:256, :], rim_low[...])
    parts[1] = (totals[1] + by_grad).T.reshape(TILE)

    pair = remote(parts.at[1 - k], partner_part, sems.at[0], sems.at[1], partner)
    pair.start()
    pl.semaphore_wait(met.at[1], 3)
    pair.wait()
    chip_sum[...] = parts[k] + partner_part[...]

    def scatter(t, slot):
        device, chip = chip_at(t)
        remote(chip_sum.at[chip], landing.at[slot], sems.at[2], sems.at[3], device).start()

    others(scatter)

    mixed[0] = mixed[0] + north
    mixed[ROWS - 1] = mixed[ROWS - 1] + south
    for i in range(ROWS):
        mixed[i, 0:1, :] = mixed[i, 0:1, :] + west[i : i + 1]
        mixed[i, COLS - 1 : COLS, :] = mixed[i, COLS - 1 : COLS, :] + east[i : i + 1]

    def settle(i, _):
        cell = pl.ds(pl.multiple_of(i * COLS, COLS), COLS)
        mixed_pair[cell, 0:256], mixed_pair[cell, 256:512] = halves(mixed[i])

    lax.fori_loop(0, ROWS, settle, None)

    pltpu.make_async_copy(landing, landing, sems.at[3]).wait()
    sums[k, me] = chip_sum[me] + jnp.sum(landing[...], axis=0)

    def gather(t, slot):
        device, _ = chip_at(t)
        remote(sums.at[k, me], sums.at[k, me], sems.at[4], sems.at[5], device).start()

    others(gather)

    for copy in (*g_copies, *l_copies):
        copy.wait_recv()
    clear_outside(gn, gs)
    for side in range(2):
        for start, value in ((NORTH + side * COLS, gn[side]), (WEST + side * STRIP, gs[side])):
            cell = slice(start, start + value.shape[0])
            grads_high[cell, :], grads_low[cell, :] = halves(value)
    near = [lab_near[i].astype(jnp.float32) for i in range(8)]
    lab_square[0:1, 0:COLS] = jnp.where(r > 0, near[0][ROWS - 1 : ROWS], -1.0)
    lab_square[1:2, 0:COLS] = jnp.where(r < GRID_ROWS - 1, near[1][0:1], -1.0)
    by_column = lab_square[...].T
    ones[NORTH : NORTH + COLS, :] = onehot(by_column[0:COLS, 0:1], COLS)
    ones[SOUTH : SOUTH + COLS, :] = onehot(by_column[0:COLS, 1:2], COLS)
    for side, column, inside in ((0, COLS - 1, c > 0), (1, 0, c < GRID_COLS - 1)):
        place_of = slice(column, column + 1)
        upper, beside_us, lower = near[4 + side], near[2 + side], near[6 + side]
        strip = jnp.concatenate(
            [
                jnp.where(
                    inside & (r > 0),
                    jnp.broadcast_to(upper[ROWS - 1 : ROWS, place_of], (8, 128)),
                    -1.0,
                ),
                jnp.where(inside, jnp.broadcast_to(beside_us[:, place_of], (ROWS, 128)), -1.0),
                jnp.where(
                    inside & (r < GRID_ROWS - 1),
                    jnp.broadcast_to(lower[0:1, place_of], (8, 128)),
                    -1.0,
                ),
                jnp.full((8, 128), -1.0, jnp.float32),
            ],
            axis=0,
        )
        cell = slice(WEST + side * STRIP, WEST + (side + 1) * STRIP)
        ones[cell, :] = onehot(strip[:, 0:1], STRIP)

    pltpu.make_async_copy(landing, landing, sems.at[5]).wait()
    back = remote(sums.at[k], sums.at[k], sems.at[6], sems.at[7], partner)
    back.start()
    pltpu.make_async_copy(landing, landing, sems.at[2]).wait()
    pltpu.make_async_copy(landing, landing, sems.at[4]).wait()
    for copy in (*f_copies, *g_copies, *l_copies):
        copy.wait_send()
    back.wait()


def apply_kernel(
    sums,
    mixed_pair,
    grads_high,
    grads_low,
    ones,
    value_weight,
    key_weight,
    centers,
    gain,
    taps,
    new_centers,
    logits,
    grad_features,
    grad_centers,
    grad_value,
    grad_key,
    new_out,
    logits_out,
    features_out,
    centers_out,
    value_out,
    key_out,
    forth,
    back_pair,
    dm,
    ds,
    small,
    wide,
    grid,
):
    by_label, by_grad = sums[0].reshape(COUNT, CHANS), sums[1].reshape(COUNT, CHANS)
    totals = precise(by_label, value_weight[...])
    centred = totals - jnp.mean(totals, axis=1, keepdims=True)
    inverse = lax.rsqrt(jnp.mean(centred * centred, axis=1, keepdims=True) + 1e-05)
    normed = centred * inverse
    new_out[...] = centers[...] + gain[...] * normed
    copies = [pltpu.make_async_copy(new_out, new_centers, small.at[0])]
    copies[-1].start()
    back = precise(new_out[...], key_weight[...], ((1,), (1,))) * SCALE
    back_high, back_low = halves(back)
    forth_high, forth_low = halves(back.T)
    forth[0:256, :] = forth_high
    forth[256:512, :] = forth_high
    forth[512:768, :] = forth_low
    for n in range(3):
        cell = slice(768 * n, 768 * (n + 1))
        out = product(mixed_pair[cell, :], forth[0:512, :]) + product(
            mixed_pair[cell, 0:256], forth[512:768, :]
        )
        logits_out[8 * n : 8 * (n + 1)] = out.reshape(8, COLS, COUNT)
        copies.append(
            pltpu.make_async_copy(
                logits_out.at[pl.ds(8 * n, 8)], logits.at[pl.ds(8 * n, 8)], wide.at[n]
            )
        )
        copies[-1].start()

    centers_out[...] = precise(by_grad, key_weight[...]) * SCALE
    copies.append(pltpu.make_async_copy(centers_out, grad_centers, small.at[1]))
    copies[-1].start()
    dnorm = centers_out[...] * gain[...]
    dsums = inverse * (
        dnorm
        - jnp.mean(dnorm, axis=1, keepdims=True)
        - normed * jnp.mean(dnorm * normed, axis=1, keepdims=True)
    )
    spread = precise(dsums, value_weight[...], ((1,), (1,)))
    spread_high, spread_low = halves(spread)
    back_pair[0:512] = spread_high
    back_pair[512:1024] = spread_low
    back_pair[1024:1536] = back_high
    back_pair[1536:2048] = back_low

    def dmixed(start, size):
        cell = slice(start, start + size)
        return (
            product(ones[cell, :], back_pair[0:512, :])
            + product(ones[cell, :], back_pair[512:1024, :])
            + product(grads_high[cell, :], back_pair[1024:1536, :])
            + product(grads_low[cell, :], back_pair[1024:1536, :])
            + product(grads_high[cell, :], back_pair[1536:2048, :])
        )

    rim = dmixed(NORTH, FULL - CELLS)
    dm[0] = rim[0:COLS]
    dm[1 + ROWS] = rim[COLS : 2 * COLS]
    ds[0] = rim[2 * COLS : 2 * COLS + STRIP]
    ds[1] = rim[2 * COLS + STRIP :]
    for n in range(3):
        dm[1 + 8 * n : 9 + 8 * n] = dmixed(768 * n, 768).reshape(8, COLS, CHANS)
    value_out[...] = precise(by_label, dsums, ((0,), (0,)))
    key_out[...] = precise(by_grad, new_out[...], ((0,), (0,))) * SCALE
    copies.append(pltpu.make_async_copy(value_out, grad_value, small.at[2]))
    copies[-1].start()
    copies.append(pltpu.make_async_copy(key_out, grad_key, small.at[3]))
    copies[-1].start()

    tap = [taps[2 - n // 3, 2 - n % 3 : 3 - n % 3] for n in range(9)]
    ds[0, 8 : 8 + ROWS, :], ds[1, 8 : 8 + ROWS, :] = (
        strip_sum(ds.at[0], [tap[3 * a] for a in range(3)]),
        strip_sum(ds.at[1], [tap[3 * a + 2] for a in range(3)]),
    )

    def unmix(i, _):
        above, here, below = dm[i], dm[i + 1], dm[i + 2]
        t = [tap[b] * above + tap[3 + b] * here + tap[6 + b] * below for b in range(3)]
        west, east = ds[0, pl.ds(8 + i, 1), :], ds[1, pl.ds(8 + i, 1), :]
        features_out[i] = here + t[1] + later(t[0], west) + earlier(t[2], east)

    for n in range(3):
        lax.fori_loop(8 * n, 8 * (n + 1), unmix, None)
        copies.append(
            pltpu.make_async_copy(
                features_out.at[pl.ds(8 * n, 8)], grad_features.at[pl.ds(8 * n, 8)], grid.at[n]
            )
        )
        copies[-1].start()
    for copy in copies:
        copy.wait()


def shards(
    features, depth_kernel, value_weight, key_weight, centers, center_gain, labels, cotangent
):
    f32, b16, vm, dma = jnp.float32, jnp.bfloat16, pltpu.VMEM, pltpu.SemaphoreType.DMA
    features, cotangent, labels, taps = (
        pltpu.with_memory_space_constraint(value, pltpu.HBM)
        for value in (features, cotangent, labels, depth_kernel)
    )
    held = pl.pallas_call(
        reduce_kernel,
        out_shape=(
            vm((2, *TILE), f32),
            vm((CELLS, 2 * CHANS), b16),
            vm((FULL, COUNT), b16),
            vm((FULL, COUNT), b16),
            vm((FULL, COUNT), b16),
        ),
        in_specs=[OUTSIDE] * 4,
        out_specs=[WHOLE] * 5,
        scratch_shapes=[
            vm((2 + ROWS, COLS, CHANS), f32),
            vm((ROWS, COLS, COUNT), f32),
            vm((ROWS, COLS), jnp.int32),
            vm((3, 3, CHANS), f32),
            vm((2, COLS, CHANS), f32),
            vm((2, COLS, COUNT), f32),
            vm((2, STRIP, CHANS), f32),
            vm((2, STRIP, COUNT), f32),
            vm((2, ROWS, CHANS), f32),
            vm((2, ROWS, COUNT), f32),
            vm((4, 8, CHANS), f32),
            vm((4, 8, COUNT), f32),
            vm((8, ROWS, COLS), jnp.int32),
            vm((128, 128), f32),
            vm((ROWS, COLS, CHANS), f32),
            vm((2 * CHANS, CELLS), b16),
            vm((2 * CHANS, 256), b16),
            vm((256, COUNT), b16),
            vm((256, COUNT), b16),
            vm((256, COUNT), b16),
            vm((2, CHANS, COUNT), f32),
            vm((2, *TILE), f32),
            vm(TILE, f32),
            vm(TILE, f32),
            vm((63, 8, 256), f32),
            dma((8,)),
            pltpu.SemaphoreType.REGULAR((2,)),
            dma((8,)),
            *[dma((8,))] * 6,
        ],
        compiler_params=pltpu.CompilerParams(
            collective_id=0, has_side_effects=True, vmem_limit_bytes=30 * 2**20
        ),
    )(features, cotangent, labels, taps)
    return pl.pallas_call(
        apply_kernel,
        out_shape=(
            jax.ShapeDtypeStruct((COUNT, CHANS), f32),
            jax.ShapeDtypeStruct((ROWS, COLS, COUNT), f32),
            jax.ShapeDtypeStruct((ROWS, COLS, CHANS), f32),
            jax.ShapeDtypeStruct((COUNT, CHANS), f32),
            jax.ShapeDtypeStruct((CHANS, CHANS), f32),
            jax.ShapeDtypeStruct((CHANS, CHANS), f32),
        ),
        in_specs=[WHOLE] * 10,
        out_specs=[OUTSIDE] * 6,
        scratch_shapes=[
            vm((COUNT, CHANS), f32),
            vm((ROWS, COLS, COUNT), f32),
            vm((ROWS, COLS, CHANS), f32),
            vm((COUNT, CHANS), f32),
            vm((CHANS, CHANS), f32),
            vm((CHANS, CHANS), f32),
            vm((768, COUNT), b16),
            vm((2048, CHANS), b16),
            vm((2 + ROWS, COLS, CHANS), f32),
            vm((2, STRIP, CHANS), f32),
            dma((4,)),
            dma((3,)),
            dma((3,)),
        ],
        compiler_params=pltpu.CompilerParams(vmem_limit_bytes=30 * 2**20),
    )(*held, value_weight, key_weight, centers, center_gain.reshape(1, CHANS), depth_kernel)


def solution(mesh):
    return jax.shard_map(
        shards,
        mesh=mesh,
        in_specs=(
            P("row", "col", None),
            P(),
            P(),
            P(),
            P(),
            P(),
            P("row", "col"),
            P("row", "col", None),
        ),
        out_specs=(P(), P("row", "col", None), P("row", "col", None), P(), P(), P()),
        check_vma=False,
    )
```

time: 120 us -> 52.4 us (0.44); the launches traced: 119 us -> 52.3 us
  matrix products: 29.5 us -> 0 us
  starting transfers between devices: 22.1 us -> 0 us
  other arithmetic: 17.5 us -> 0 us
  Pallas kernels: 34.1 us -> 51.5 us
  local copies, waits for them, and re-layouts: 9.78 us -> 0.02 us
  waiting for transfers between devices: 4.47 us -> 0 us
    dot_general x11 -> x0, matrix products: 29.5 us -> none  [the longest x7 18.6 us: matmul(): jnp.dot(left, right, preferred_element_type=jnp.float32, precision=lax.Pr...]
    ppermute x8 -> x0, starting transfers between devices: 22.1 us -> none  [the longest x4 14.4 us: padded_2(): lax.ppermute(tail, axis, [(i, (i + 1) % count) for i in range(ends)])]
    pallas_call x1 -> x2, Pallas kernels: 34.1 us -> 51.5 us  [the longest x1 40.1 us: shards(): pl.pallas_call(reduce_kernel, out_shape=(vm((2, *TILE), f32), vm((CELLS,...]
    add x2 -> x0, other arithmetic: 14.2 us -> none  [the longest x1 10.1 us: shards(): mixed = mixed + depth_kernel[a, b] * padded[a:a + rows, b:b + cols]]
    unnamed x50 -> x10, local copies, waits for them, and re-layouts: 5.56 us -> 0.02 us
    ppermute x8 -> x0, waiting for transfers between devices: 4.47 us -> none  [the longest x4 4.46 us: padded_2(): lax.ppermute(head, axis, [((i + 1) % count, i) for i in range(ends)])]
    dot_general x2 -> x0, local copies, waits for them, and re-layouts: 2.23 us -> none  [the longest x1 1.24 us: inner_rows(): lax.dot_general(left, right, (((0,), (0,)), ((), ())), preferred_element_...]
    slice x4 -> x0, local copies, waits for them, and re-layouts: 1.91 us -> none  [the longest x1 1 us: padded_2(): head = lax.slice_in_dim(cells, 0, width, axis=dim)]
  transfers between devices with their start and end apart: 8 -> 0, of which waited for: 3 -> 0; matrix products, arithmetic and copies ran while one was open for 8% -> 0% of each run, Pallas kernels for 0% -> 0%
where the time goes in v2:
time: 52.4 us; the launch traced here: 52.3 us
  Pallas kernels  51.5 us (98%)
  between operations  0.72 us (1%)
    pallas_call x1, Pallas kernels, shards(): pl.pallas_call(reduce_kernel, out_shape=(vm((2, *TILE), f32), vm((CELLS,...  40.1 us
    pallas_call x1, Pallas kernels, shards(): pl.pallas_call(apply_kernel, out_shape=(jax.ShapeDtypeStruct((COUNT, CHAN...  11.4 us

profile of v2, /device:TPU:1, one launch (start us, length us, event | category | flops | bytes accessed | tf_op | source)
XLA Modules:
  0.0 52.3 jit_solution(13471747551122487785)
XLA Ops:
  0.6 0.0 copy-start
  0.6 0.0 copy-start.1
  0.7 0.0 copy-start.2
  0.7 0.0 copy-start.3
  0.7 0.0 copy-start.4
  0.7 40.1 %shard_map.127 = (f32[2,64,8,256]{3,2,1,0:T(8,128)S(1)}, bf16[2304,512]{1,0:T(8,128)(2,1)S(1)}, bf16[2592,512]{1,0:T(8,128)(2,1)S(1)}, bf16[2592,512]{1,0:T(8,128)(2,1)S(1)}, bf16[2592,512]{1,0:T(8,128)(2,1)S(1)}) custom-call(f32[24,96,256]{2,1,0:T(8,128)} %features.1, f32[24,96,512]{2,1,0:T(8,128)} %cotangent.1, s32[24,96]{1,0:T(8,128)} %labels.1, ...), custom_call_target="tpu_custom_call" | custom-call | tf_op jit(solution)/shard_map/pallas_call | solution.py:516
  40.8 0.0 copy-done
  40.8 0.0 copy-done.1
  40.8 0.0 copy-done.2
  40.8 0.0 copy-done.3
  40.8 0.0 copy-done.4
  40.8 11.4 %shard_map.128 = (f32[512,256]{1,0:T(8,128)}, f32[24,96,512]{2,1,0:T(8,128)}, f32[24,96,256]{2,1,0:T(8,128)}, f32[512,256]{1,0:T(8,128)}, f32[256,256]{1,0:T(8,128)}, /*index=5*/f32[256,256]{1,0:T(8,128)}) custom-call(f32[2,64,8,256]{3,2,1,0:T(8,128)S(1)} %get-tuple-element.11.sums, bf16[2304,512]{1,0:T(8,128)(2,1)S(1)} %get-tuple-element.12.mixed_pair, ...), custom_call_target="tpu_custom_call" | custom-call | tf_op jit(solution)/shard_map/pallas_call | solution.py:562
Async XLA Ops:
  0.6 40.2 %copy-start = (f32[512,256]{1,0:T(8,128)S(1)}, f32[512,256]{1,0:T(8,128)}, u32[]{:S(2)}) copy-start(f32[512,256]{1,0:T(8,128)} %centers.1) | copy-start | bytes 1572868
  0.6 40.2 %copy-start.1 = (f32[256,256]{1,0:T(8,128)S(1)}, f32[256,256]{1,0:T(8,128)}, u32[]{:S(2)}) copy-start(f32[256,256]{1,0:T(8,128)} %value_weight.1) | copy-start | bytes 786436
  0.7 40.2 %copy-start.2 = (f32[256,256]{1,0:T(8,128)S(1)}, f32[256,256]{1,0:T(8,128)}, u32[]{:S(2)}) copy-start(f32[256,256]{1,0:T(8,128)} %key_weight.1) | copy-start | bytes 786436
  0.7 40.2 %copy-start.3 = (f32[3,3,256]{2,1,0:T(4,128)S(1)}, f32[3,3,256]{2,1,0:T(4,128)}, u32[]{:S(2)}) copy-start(f32[3,3,256]{2,1,0:T(4,128)} %taps.1) | copy-start | bytes 27652
  0.7 40.2 %copy-start.4 = (f32[256]{0:T(256)S(1)}, f32[256]{0:T(256)}, u32[]{:S(2)}) copy-start(f32[256]{0:T(256)} %param.13) | copy-start | bytes 3076

commit v3 on v2

--- a/solution.py
+++ b/solution.py
@@ -14,7 +14,12 @@
 NORTH, SOUTH, WEST, EAST = CELLS, CELLS + COLS, CELLS + 2 * COLS, CELLS + 2 * COLS + STRIP
 FULL = CELLS + 2 * COLS + 2 * STRIP
 SCALE = 1.0 / 16.0
-SELF = 42
+ONES, UPPER, LOWER = slice(0, 512), slice(512, 1024), slice(1024, 1536)
+ORDER = (
+    42, 38, 46, 41, 43, 58, 26, 37, 59, 25, 39, 34, 22, 62, 54, 47, 57, 40, 30, 45, 27,
+    10, 9, 55, 29, 31, 14, 61, 50, 53, 18, 21, 35, 24, 56, 44, 11, 33, 23, 6, 36, 63,
+    52, 49, 5, 17, 8, 32, 7, 2, 28, 15, 51, 60, 13, 19, 20, 1, 48, 16, 12, 4, 3,
+)
 TILE = (64, 8, 256)
 SIDES = ((-1, 0), (1, 0), (0, -1), (0, 1), (-1, -1), (-1, 1), (1, -1), (1, 1))
 OPPOSITE = (1, 0, 3, 2, 7, 6, 5, 4)
@@ -31,11 +36,16 @@
     return (lax.rem(x, 4) * 4 + lax.rem(y, 4), lax.rem(z, 4) * 2 + k)
 
 
-def chip_at(t):
+def chip_at(code):
     x, y, z, k = place()
-    x, y, z = x + t // 16 + 2, y + lax.rem(t // 4, 4) + 2, z + lax.rem(t, 4) + 2
+    x, y, z = x + code // 16, y + code // 4 % 4, z + code % 4
     x, y, z = lax.rem(x, 4), lax.rem(y, 4), lax.rem(z, 4)
     return (x * 4 + y, z * 2 + k), x * 16 + y * 4 + z
+
+
+def opposite(code):
+    x, y, z = code // 16, code // 4 % 4, code % 4
+    return -x % 4 * 16 + -y % 4 * 4 + -z % 4
 
 
 def signal(sem, device):
@@ -46,11 +56,6 @@
     return pltpu.make_async_remote_copy(
         src_ref=src, dst_ref=dst, send_sem=send, recv_sem=recv, device_id=device, device_id_type=MESH
     )
-
-
-def others(step):
-    lax.fori_loop(0, SELF, lambda t, _: step(t, t), None)
-    lax.fori_loop(SELF + 1, 64, lambda t, _: step(t, t - 1), None)
 
 
 def halves(value):
@@ -152,9 +157,7 @@
     taps_in,
     sums,
     mixed_pair,
-    grads_high,
-    grads_low,
-    ones,
+    acts,
     fx,
     gx,
     lab,
@@ -172,9 +175,7 @@
     mixed,
     mixed_t,
     rim_t,
-    rim_ones,
-    rim_high,
-    rim_low,
+    rim_acts,
     totals,
     parts,
     partner_part,
@@ -183,6 +184,7 @@
     load,
     met,
     sems,
+    got,
     f_send,
     f_recv,
     g_send,
@@ -226,67 +228,87 @@
     lab_square[0:ROWS, 0:COLS] = lab[...].astype(jnp.float32)
     by_column = lab_square[...].T
     for i in range(ROWS):
-        ones[COLS * i : COLS * (i + 1), :] = onehot(by_column[0:COLS, i : i + 1], COLS)
+        acts[COLS * i : COLS * (i + 1), ONES] = onehot(by_column[0:COLS, i : i + 1], COLS)
     for copy in load_f:
         copy.wait()
     pack(fx, f_ends, f_corners, 1)
-    for copy in load_g:
-        copy.wait()
-    pack(gx, g_ends, g_corners, 0)
-    pl.semaphore_wait(barrier, 10 + len(SIDES))
     f_copies = halo_copies(fx, fn, fs, f_ends, f_corners, f_send, f_recv, 1)
     g_copies = halo_copies(gx, gn, gs, g_ends, g_corners, g_send, g_recv, 0)
     l_copies = [
         remote(lab, lab_near.at[OPPOSITE[i]], l_send.at[i], l_recv.at[i], beside(*side))
         for i, side in enumerate(SIDES)
     ]
+    tap = [taps[n // 3, n % 3 : n % 3 + 1] for n in range(9)]
+
+    def mix(n):
+        for i in range(8 * n, 8 * (n + 1)):
+            above, here, below = fx[i], fx[i + 1], fx[i + 2]
+            t = [tap[b] * above + tap[3 + b] * here + tap[6 + b] * below for b in range(3)]
+            mixed[i] = here + t[1] + later(t[0]) + earlier(t[2])
+        block = mixed[8 * n : 8 * (n + 1)].reshape(768, CHANS)
+        for m in range(3):
+            cell = slice(768 * n + 256 * m, 768 * n + 256 * (m + 1))
+            mixed_t[0:256, cell], mixed_t[256:512, cell] = halves(
+                block[256 * m : 256 * (m + 1)].T
+            )
+
+    def split(n):
+        for i in range(8 * n, 8 * (n + 1)):
+            cell = slice(COLS * i, COLS * (i + 1))
+            acts[cell, UPPER], acts[cell, LOWER] = halves(gx[i])
+
+    def add(which, n, value):
+        totals[which] = value if n == 0 else totals[which] + value
+
+    def sum_labels(n):
+        cell = slice(768 * n, 768 * (n + 1))
+        value = product(mixed_t[:, cell], acts[cell, ONES])
+        add(0, n, value[0:256] + value[256:512])
+
+    def sum_grads(n):
+        cell = slice(768 * n, 768 * (n + 1))
+        value = product(mixed_t[:, cell], acts[cell, UPPER])
+        more = product(mixed_t[0:256, cell], acts[cell, LOWER])
+        add(1, n, value[0:256] + value[256:512] + more)
+
+    mix(0)
+    sum_labels(0)
+    mix(1)
+    pl.semaphore_wait(barrier, 10 + len(SIDES))
     for copy in f_copies:
         copy.start()
     for device in lines[0]:
         signal(met.at[0], device)
-    for copy in (*g_copies, *l_copies):
+    for copy in l_copies:
         copy.start()
-
-    tap = [taps[n // 3, n % 3 : n % 3 + 1] for n in range(9)]
-
-    def mix(i, _):
-        above, here, below = fx[i], fx[i + 1], fx[i + 2]
-        t = [
-            tap[b] * above + tap[3 + b] * here + tap[6 + b] * below for b in range(3)
-        ]
-        mixed[i] = here + t[1] + later(t[0]) + earlier(t[2])
-        cell = pl.ds(pl.multiple_of(i * COLS, COLS), COLS)
-        grads_high[cell, :], grads_low[cell, :] = halves(gx[i])
-
-    lax.fori_loop(0, ROWS, mix, None)
-    for n in range(9):
-        block = mixed[...].reshape(CELLS, CHANS)[256 * n : 256 * (n + 1)].T
-        mixed_t[0:256, 256 * n : 256 * (n + 1)], mixed_t[256:512, 256 * n : 256 * (n + 1)] = halves(
-            block
-        )
+    sum_labels(1)
+    mix(2)
+    for copy in load_g:
+        copy.wait()
+    pack(gx, g_ends, g_corners, 0)
+    for copy in g_copies:
+        copy.start()
+    sum_labels(2)
+    split(0)
+    sum_grads(0)
+    split(1)
+    sum_grads(1)
+    split(2)
     pl.semaphore_wait(met.at[0], 3)
     for device in lines[1]:
         signal(met.at[1], device)
-    by_label = product(mixed_t[...], ones[0:CELLS, :])
-    totals[0] = by_label[0:256] + by_label[256:512]
-    by_grad = product(mixed_t[...], grads_high[0:CELLS, :])
-    totals[1] = (
-        by_grad[0:256] + by_grad[256:512] + product(mixed_t[0:256, :], grads_low[0:CELLS, :])
-    )
-
-    rim_ones[...] = jnp.zeros_like(rim_ones)
-    rim_high[...] = jnp.zeros_like(rim_high)
-    rim_low[...] = jnp.zeros_like(rim_low)
-    for rim, own in ((rim_ones, ones), (rim_high, grads_high), (rim_low, grads_low)):
-        rim[0:COLS, :] = own[0:COLS, :]
-        rim[COLS : 2 * COLS, :] = own[CELLS - COLS : CELLS, :]
+    sum_grads(2)
+
+    rim_acts[...] = jnp.zeros_like(rim_acts)
+    rim_acts[0:COLS, :] = acts[0:COLS, :]
+    rim_acts[COLS : 2 * COLS, :] = acts[CELLS - COLS : CELLS, :]
     fill = jnp.zeros((8, COUNT), jnp.float32)
     for side, column in ((0, 0), (1, COLS - 1)):
         cell = slice(192 + 32 * side, 224 + 32 * side)
-        rim_high[cell, :], rim_low[cell, :] = halves(
+        rim_acts[cell, UPPER], rim_acts[cell, LOWER] = halves(
             jnp.concatenate([g_ends[side], fill], axis=0)
         )
-        rim_ones[cell, :] = onehot(lab_square[0:32, column : column + 1], 32)
+        rim_acts[cell, ONES] = onehot(lab_square[0:32, column : column + 1], 32)
 
     for copy in f_copies:
         copy.wait_recv()
@@ -298,10 +320,10 @@
     gap = jnp.zeros((8, CHANS), jnp.float32)
     rim = jnp.concatenate([north, south, west, gap, east, gap], axis=0)
     rim_t[0:256, :], rim_t[256:512, :] = halves(rim.T)
-    by_label = product(rim_t[...], rim_ones[...])
+    by_label = product(rim_t[...], rim_acts[:, ONES])
     parts[0] = (totals[0] + by_label[0:256] + by_label[256:512]).T.reshape(TILE)
-    by_grad = product(rim_t[...], rim_high[...])
-    by_grad = by_grad[0:256] + by_grad[256:512] + product(rim_t[0:256, :], rim_low[...])
+    by_grad = product(rim_t[...], rim_acts[:, UPPER])
+    by_grad = by_grad[0:256] + by_grad[256:512] + product(rim_t[0:256, :], rim_acts[:, LOWER])
     parts[1] = (totals[1] + by_grad).T.reshape(TILE)
 
     pair = remote(parts.at[1 - k], partner_part, sems.at[0], sems.at[1], partner)
@@ -310,11 +332,9 @@
     pair.wait()
     chip_sum[...] = parts[k] + partner_part[...]
 
-    def scatter(t, slot):
-        device, chip = chip_at(t)
+    for slot, code in enumerate(ORDER):
+        device, chip = chip_at(code)
         remote(chip_sum.at[chip], landing.at[slot], sems.at[2], sems.at[3], device).start()
-
-    others(scatter)
 
     mixed[0] = mixed[0] + north
     mixed[ROWS - 1] = mixed[ROWS - 1] + south
@@ -331,11 +351,9 @@
     pltpu.make_async_copy(landing, landing, sems.at[3]).wait()
     sums[k, me] = chip_sum[me] + jnp.sum(landing[...], axis=0)
 
-    def gather(t, slot):
-        device, _ = chip_at(t)
-        remote(sums.at[k, me], sums.at[k, me], sems.at[4], sems.at[5], device).start()
-
-    others(gather)
+    for slot, code in enumerate(ORDER):
+        device, _ = chip_at(code)
+        remote(sums.at[k, me], sums.at[k, me], sems.at[4], got.at[slot // 21], device).start()
 
     for copy in (*g_copies, *l_copies):
         copy.wait_recv()
@@ -343,13 +361,13 @@
     for side in range(2):
         for start, value in ((NORTH + side * COLS, gn[side]), (WEST + side * STRIP, gs[side])):
             cell = slice(start, start + value.shape[0])
-            grads_high[cell, :], grads_low[cell, :] = halves(value)
+            acts[cell, UPPER], acts[cell, LOWER] = halves(value)
     near = [lab_near[i].astype(jnp.float32) for i in range(8)]
     lab_square[0:1, 0:COLS] = jnp.where(r > 0, near[0][ROWS - 1 : ROWS], -1.0)
     lab_square[1:2, 0:COLS] = jnp.where(r < GRID_ROWS - 1, near[1][0:1], -1.0)
     by_column = lab_square[...].T
-    ones[NORTH : NORTH + COLS, :] = onehot(by_column[0:COLS, 0:1], COLS)
-    ones[SOUTH : SOUTH + COLS, :] = onehot(by_column[0:COLS, 1:2], COLS)
+    acts[NORTH : NORTH + COLS, ONES] = onehot(by_column[0:COLS, 0:1], COLS)
+    acts[SOUTH : SOUTH + COLS, ONES] = onehot(by_column[0:COLS, 1:2], COLS)
     for side, column, inside in ((0, COLS - 1, c > 0), (1, 0, c < GRID_COLS - 1)):
         place_of = slice(column, column + 1)
         upper, beside_us, lower = near[4 + side], near[2 + side], near[6 + side]
@@ -371,24 +389,29 @@
             axis=0,
         )
         cell = slice(WEST + side * STRIP, WEST + (side + 1) * STRIP)
-        ones[cell, :] = onehot(strip[:, 0:1], STRIP)
-
-    pltpu.make_async_copy(landing, landing, sems.at[5]).wait()
-    back = remote(sums.at[k], sums.at[k], sems.at[6], sems.at[7], partner)
-    back.start()
+        acts[cell, ONES] = onehot(strip[:, 0:1], STRIP)
+
+    slab = sums.at[k, me]
+    remote(slab, slab, sems.at[6], sems.at[7], partner).start()
+    for group in range(3):
+        block = landing.at[pl.ds(0, 21)]
+        pltpu.make_async_copy(block, block, got.at[group]).wait()
+        for code in ORDER[21 * group : 21 * (group + 1)]:
+            _, chip = chip_at(opposite(code))
+            slab = sums.at[k, chip]
+            remote(slab, slab, sems.at[6], sems.at[7], partner).start()
     pltpu.make_async_copy(landing, landing, sems.at[2]).wait()
     pltpu.make_async_copy(landing, landing, sems.at[4]).wait()
     for copy in (*f_copies, *g_copies, *l_copies):
         copy.wait_send()
-    back.wait()
+    half = sums.at[k]
+    remote(half, half, sems.at[6], sems.at[7], partner).wait()
 
 
 def apply_kernel(
     sums,
     mixed_pair,
-    grads_high,
-    grads_low,
-    ones,
+    acts,
     value_weight,
     key_weight,
     centers,
@@ -416,34 +439,17 @@
 ):
     by_label, by_grad = sums[0].reshape(COUNT, CHANS), sums[1].reshape(COUNT, CHANS)
     totals = precise(by_label, value_weight[...])
+    centers_out[...] = precise(by_grad, key_weight[...]) * SCALE
     centred = totals - jnp.mean(totals, axis=1, keepdims=True)
     inverse = lax.rsqrt(jnp.mean(centred * centred, axis=1, keepdims=True) + 1e-05)
     normed = centred * inverse
     new_out[...] = centers[...] + gain[...] * normed
-    copies = [pltpu.make_async_copy(new_out, new_centers, small.at[0])]
-    copies[-1].start()
     back = precise(new_out[...], key_weight[...], ((1,), (1,))) * SCALE
     back_high, back_low = halves(back)
     forth_high, forth_low = halves(back.T)
     forth[0:256, :] = forth_high
     forth[256:512, :] = forth_high
     forth[512:768, :] = forth_low
-    for n in range(3):
-        cell = slice(768 * n, 768 * (n + 1))
-        out = product(mixed_pair[cell, :], forth[0:512, :]) + product(
-            mixed_pair[cell, 0:256], forth[512:768, :]
-        )
-        logits_out[8 * n : 8 * (n + 1)] = out.reshape(8, COLS, COUNT)
-        copies.append(
-            pltpu.make_async_copy(
-                logits_out.at[pl.ds(8 * n, 8)], logits.at[pl.ds(8 * n, 8)], wide.at[n]
-            )
-        )
-        copies[-1].start()
-
-    centers_out[...] = precise(by_grad, key_weight[...]) * SCALE
-    copies.append(pltpu.make_async_copy(centers_out, grad_centers, small.at[1]))
-    copies[-1].start()
     dnorm = centers_out[...] * gain[...]
     dsums = inverse * (
         dnorm
@@ -453,54 +459,69 @@
     spread = precise(dsums, value_weight[...], ((1,), (1,)))
     spread_high, spread_low = halves(spread)
     back_pair[0:512] = spread_high
-    back_pair[512:1024] = spread_low
+    back_pair[512:1024] = back_high
     back_pair[1024:1536] = back_high
-    back_pair[1536:2048] = back_low
+    back_pair[1536:2048] = spread_low
+    back_pair[2048:2560] = back_low
+    copies = []
+
+    def send(out, to, sem):
+        copies.append(pltpu.make_async_copy(out, to, sem))
+        copies[-1].start()
+
+    def project(n):
+        cell = slice(384 * n, 384 * (n + 1))
+        out = product(mixed_pair[cell, :], forth[0:512, :]) + product(
+            mixed_pair[cell, 0:256], forth[512:768, :]
+        )
+        logits_out[4 * n : 4 * (n + 1)] = out.reshape(4, COLS, COUNT)
 
     def dmixed(start, size):
         cell = slice(start, start + size)
-        return (
-            product(ones[cell, :], back_pair[0:512, :])
-            + product(ones[cell, :], back_pair[512:1024, :])
-            + product(grads_high[cell, :], back_pair[1024:1536, :])
-            + product(grads_low[cell, :], back_pair[1024:1536, :])
-            + product(grads_high[cell, :], back_pair[1536:2048, :])
+        return product(acts[cell, :], back_pair[0:1536, :]) + product(
+            acts[cell, 0:1024], back_pair[1536:2560, :]
         )
 
+    def spread_cells(n):
+        dm[1 + 4 * n : 5 + 4 * n] = dmixed(384 * n, 384).reshape(4, COLS, CHANS)
+
+    tap = [taps[2 - n // 3, 2 - n % 3 : 3 - n % 3] for n in range(9)]
+
+    def unmix(n):
+        for i in range(4 * n, 4 * (n + 1)):
+            above, here, below = dm[i], dm[i + 1], dm[i + 2]
+            t = [tap[b] * above + tap[3 + b] * here + tap[6 + b] * below for b in range(3)]
+            west, east = west_rim[i : i + 1], east_rim[i : i + 1]
+            features_out[i] = here + t[1] + later(t[0], west) + earlier(t[2], east)
+
+    for n in range(6):
+        project(n)
+        if n % 2:
+            rows = pl.ds(4 * (n - 1), 8)
+            send(logits_out.at[rows], logits.at[rows], wide.at[n // 2])
+    send(new_out, new_centers, small.at[0])
+    send(centers_out, grad_centers, small.at[1])
     rim = dmixed(NORTH, FULL - CELLS)
     dm[0] = rim[0:COLS]
     dm[1 + ROWS] = rim[COLS : 2 * COLS]
     ds[0] = rim[2 * COLS : 2 * COLS + STRIP]
     ds[1] = rim[2 * COLS + STRIP :]
-    for n in range(3):
-        dm[1 + 8 * n : 9 + 8 * n] = dmixed(768 * n, 768).reshape(8, COLS, CHANS)
-    value_out[...] = precise(by_label, dsums, ((0,), (0,)))
-    key_out[...] = precise(by_grad, new_out[...], ((0,), (0,))) * SCALE
-    copies.append(pltpu.make_async_copy(value_out, grad_value, small.at[2]))
-    copies[-1].start()
-    copies.append(pltpu.make_async_copy(key_out, grad_key, small.at[3]))
-    copies[-1].start()
-
-    tap = [taps[2 - n // 3, 2 - n % 3 : 3 - n % 3] for n in range(9)]
-    ds[0, 8 : 8 + ROWS, :], ds[1, 8 : 8 + ROWS, :] = (
-        strip_sum(ds.at[0], [tap[3 * a] for a in range(3)]),
-        strip_sum(ds.at[1], [tap[3 * a + 2] for a in range(3)]),
-    )
-
-    def unmix(i, _):
-        above, here, below = dm[i], dm[i + 1], dm[i + 2]
-        t = [tap[b] * above + tap[3 + b] * here + tap[6 + b] * below for b in range(3)]
-        west, east = ds[0, pl.ds(8 + i, 1), :], ds[1, pl.ds(8 + i, 1), :]
-        features_out[i] = here + t[1] + later(t[0], west) + earlier(t[2], east)
-
-    for n in range(3):
-        lax.fori_loop(8 * n, 8 * (n + 1), unmix, None)
-        copies.append(
-            pltpu.make_async_copy(
-                features_out.at[pl.ds(8 * n, 8)], grad_features.at[pl.ds(8 * n, 8)], grid.at[n]
-            )
-        )
-        copies[-1].start()
+    west_rim = strip_sum(ds.at[0], [tap[3 * a] for a in range(3)])
+    east_rim = strip_sum(ds.at[1], [tap[3 * a + 2] for a in range(3)])
+    spread_cells(0)
+    spread_cells(1)
+    for n in range(6):
+        unmix(n)
+        if n < 4:
+            spread_cells(n + 2)
+        if n == 4:
+            value_out[...] = precise(by_label, dsums, ((0,), (0,)))
+            key_out[...] = precise(by_grad, new_out[...], ((0,), (0,))) * SCALE
+            send(value_out, grad_value, small.at[2])
+            send(key_out, grad_key, small.at[3])
+        if n % 2:
+            rows = pl.ds(4 * (n - 1), 8)
+            send(features_out.at[rows], grad_features.at[rows], grid.at[n // 2])
     for copy in copies:
         copy.wait()
 
@@ -518,12 +539,10 @@
         out_shape=(
             vm((2, *TILE), f32),
             vm((CELLS, 2 * CHANS), b16),
-            vm((FULL, COUNT), b16),
-            vm((FULL, COUNT), b16),
-            vm((FULL, COUNT), b16),
+            vm((FULL, 3 * COUNT), b16),
         ),
         in_specs=[OUTSIDE] * 4,
-        out_specs=[WHOLE] * 5,
+        out_specs=[WHOLE] * 3,
         scratch_shapes=[
             vm((2 + ROWS, COLS, CHANS), f32),
             vm((ROWS, COLS, COUNT), f32),
@@ -542,9 +561,7 @@
             vm((ROWS, COLS, CHANS), f32),
             vm((2 * CHANS, CELLS), b16),
             vm((2 * CHANS, 256), b16),
-            vm((256, COUNT), b16),
-            vm((256, COUNT), b16),
-            vm((256, COUNT), b16),
+            vm((256, 3 * COUNT), b16),
             vm((2, CHANS, COUNT), f32),
             vm((2, *TILE), f32),
             vm(TILE, f32),
@@ -553,6 +570,7 @@
             dma((8,)),
             pltpu.SemaphoreType.REGULAR((2,)),
             dma((8,)),
+            dma((3,)),
             *[dma((8,))] * 6,
         ],
         compiler_params=pltpu.CompilerParams(
@@ -569,7 +587,7 @@
             jax.ShapeDtypeStruct((CHANS, CHANS), f32),
             jax.ShapeDtypeStruct((CHANS, CHANS), f32),
         ),
-        in_specs=[WHOLE] * 10,
+        in_specs=[WHOLE] * 8,
         out_specs=[OUTSIDE] * 6,
         scratch_shapes=[
             vm((COUNT, CHANS), f32),
@@ -579,7 +597,7 @@
             vm((CHANS, CHANS), f32),
             vm((CHANS, CHANS), f32),
             vm((768, COUNT), b16),
-            vm((2048, CHANS), b16),
+            vm((2560, CHANS), b16),
             vm((2 + ROWS, COLS, CHANS), f32),
             vm((2, STRIP, CHANS), f32),
             dma((4,)),

time: 52.4 us -> 48.3 us (0.922)
  Pallas kernels: 51.5 us -> 47.3 us
    pallas_call x1, Pallas kernels: 40.1 us -> 37.9 us  [shards(): pl.pallas_call(reduce_kernel, out_shape=(vm((2, *TILE), f32), vm((CELLS,...]
    pallas_call x1, Pallas kernels: 11.4 us -> 9.42 us  [shards(): pl.pallas_call(apply_kernel, out_shape=(jax.ShapeDtypeStruct((COUNT, CHAN...]
where the time goes in v3:
time: 48.3 us; the launch traced here: 48.2 us
  Pallas kernels  47.3 us (98%)
  between operations  0.88 us (2%)
    pallas_call x1, Pallas kernels, shards(): pl.pallas_call(reduce_kernel, out_shape=(vm((2, *TILE), f32), vm((CELLS,...  37.9 us
    pallas_call x1, Pallas kernels, shards(): pl.pallas_call(apply_kernel, out_shape=(jax.ShapeDtypeStruct((COUNT, CHAN...  9.42 us

profile of v3, /device:TPU:1, one launch (start us, length us, event | category | flops | bytes accessed | tf_op | source)
XLA Modules:
  0.0 48.2 jit_solution(15780088309076461081)
XLA Ops:
  0.6 0.0 copy-start.3
  0.6 0.0 copy-start.4
  0.7 0.0 copy-start
  0.7 0.0 copy-start.2
  0.7 0.0 copy-start.1
  0.7 37.9 %shard_map.127 = (f32[2,64,8,256]{3,2,1,0:T(8,128)S(1)}, bf16[2304,512]{1,0:T(8,128)(2,1)S(1)}, bf16[2592,1536]{1,0:T(8,128)(2,1)S(1)}) custom-call(f32[24,96,256]{2,1,0:T(8,128)} %features.1, f32[24,96,512]{2,1,0:T(8,128)} %cotangent.1, s32[24,96]{1,0:T(8,128)} %labels.1, f32[3,3,256]{2,1,0:T(4,128)} %taps.1), custom_call_target="tpu_custom_call" | custom-call | tf_op jit(solution)/shard_map/pallas_call | solution.py:537
  38.6 0.0 copy-done.3
  38.6 0.0 copy-done.4
  38.6 0.0 copy-done
  38.6 0.0 copy-done.2
  38.6 0.0 copy-done.1
  38.7 9.4 %shard_map.128 = (f32[512,256]{1,0:T(8,128)}, f32[24,96,512]{2,1,0:T(8,128)}, f32[24,96,256]{2,1,0:T(8,128)}, f32[512,256]{1,0:T(8,128)}, f32[256,256]{1,0:T(8,128)}, /*index=5*/f32[256,256]{1,0:T(8,128)}) custom-call(f32[2,64,8,256]{3,2,1,0:T(8,128)S(1)} %get-tuple-element.9.sums, bf16[2304,512]{1,0:T(8,128)(2,1)S(1)} %get-tuple-element.10.mixed_pair, ...), custom_call_target="tpu_custom_call" | custom-call | tf_op jit(solution)/shard_map/pallas_call | solution.py:580
Async XLA Ops:
  0.6 38.0 %copy-start.3 = (f32[3,3,256]{2,1,0:T(4,128)S(1)}, f32[3,3,256]{2,1,0:T(4,128)}, u32[]{:S(2)}) copy-start(f32[3,3,256]{2,1,0:T(4,128)} %taps.1) | copy-start | bytes 27652
  0.6 38.0 %copy-start.4 = (f32[256]{0:T(256)S(1)}, f32[256]{0:T(256)}, u32[]{:S(2)}) copy-start(f32[256]{0:T(256)} %param.13) | copy-start | bytes 3076
  0.7 38.0 %copy-start = (f32[512,256]{1,0:T(8,128)S(1)}, f32[512,256]{1,0:T(8,128)}, u32[]{:S(2)}) copy-start(f32[512,256]{1,0:T(8,128)} %centers.1) | copy-start | bytes 1572868
  0.7 38.0 %copy-start.2 = (f32[256,256]{1,0:T(8,128)S(1)}, f32[256,256]{1,0:T(8,128)}, u32[]{:S(2)}) copy-start(f32[256,256]{1,0:T(8,128)} %key_weight.1) | copy-start | bytes 786436
  0.7 38.0 %copy-start.1 = (f32[256,256]{1,0:T(8,128)S(1)}, f32[256,256]{1,0:T(8,128)}, u32[]{:S(2)}) copy-start(f32[256,256]{1,0:T(8,128)} %value_weight.1) | copy-start | bytes 786436

commit v4 on v3

--- a/solution.py
+++ b/solution.py
@@ -353,7 +353,7 @@
 
     for slot, code in enumerate(ORDER):
         device, _ = chip_at(code)
-        remote(sums.at[k, me], sums.at[k, me], sems.at[4], got.at[slot // 21], device).start()
+        remote(sums.at[k, me], sums.at[k, me], sems.at[4], got.at[(slot >= 42) + (slot >= 56)], device).start()
 
     for copy in (*g_copies, *l_copies):
         copy.wait_recv()
@@ -393,10 +393,10 @@
 
     slab = sums.at[k, me]
     remote(slab, slab, sems.at[6], sems.at[7], partner).start()
-    for group in range(3):
-        block = landing.at[pl.ds(0, 21)]
+    for group, (start, end) in enumerate(((0, 42), (42, 56), (56, 63))):
+        block = landing.at[pl.ds(0, end - start)]
         pltpu.make_async_copy(block, block, got.at[group]).wait()
-        for code in ORDER[21 * group : 21 * (group + 1)]:
+        for code in ORDER[start:end]:
             _, chip = chip_at(opposite(code))
             slab = sums.at[k, chip]
             remote(slab, slab, sems.at[6], sems.at[7], partner).start()

time: 48.3 us -> 48.5 us (level)
  no operation moved by 1% of the time
where the time goes in v4:
time: 48.5 us; the launch traced here: 48.4 us
  Pallas kernels  47.5 us (98%)
  between operations  0.88 us (2%)
    pallas_call x1, Pallas kernels, shards(): pl.pallas_call(reduce_kernel, out_shape=(vm((2, *TILE), f32), vm((CELLS,...  38.1 us
    pallas_call x1, Pallas kernels, shards(): pl.pallas_call(apply_kernel, out_shape=(jax.ShapeDtypeStruct((COUNT, CHAN...  9.42 us

profile of v4, /device:TPU:1, one launch (start us, length us, event | category | flops | bytes accessed | tf_op | source)
XLA Modules:
  0.0 48.4 jit_solution(2597749086311485111)
XLA Ops:
  0.6 0.0 copy-start.3
  0.6 0.0 copy-start.4
  0.7 0.0 copy-start
  0.7 0.0 copy-start.2
  0.7 0.0 copy-start.1
  0.7 38.1 %shard_map.127 = (f32[2,64,8,256]{3,2,1,0:T(8,128)S(1)}, bf16[2304,512]{1,0:T(8,128)(2,1)S(1)}, bf16[2592,1536]{1,0:T(8,128)(2,1)S(1)}) custom-call(f32[24,96,256]{2,1,0:T(8,128)} %features.1, f32[24,96,512]{2,1,0:T(8,128)} %cotangent.1, s32[24,96]{1,0:T(8,128)} %labels.1, f32[3,3,256]{2,1,0:T(4,128)} %taps.1), custom_call_target="tpu_custom_call" | custom-call | tf_op jit(solution)/shard_map/pallas_call | solution.py:537
  38.8 0.0 copy-done.3
  38.8 0.0 copy-done.4
  38.8 0.0 copy-done
  38.8 0.0 copy-done.2
  38.9 0.0 copy-done.1
  38.9 9.4 %shard_map.128 = (f32[512,256]{1,0:T(8,128)}, f32[24,96,512]{2,1,0:T(8,128)}, f32[24,96,256]{2,1,0:T(8,128)}, f32[512,256]{1,0:T(8,128)}, f32[256,256]{1,0:T(8,128)}, /*index=5*/f32[256,256]{1,0:T(8,128)}) custom-call(f32[2,64,8,256]{3,2,1,0:T(8,128)S(1)} %get-tuple-element.9.sums, bf16[2304,512]{1,0:T(8,128)(2,1)S(1)} %get-tuple-element.10.mixed_pair, ...), custom_call_target="tpu_custom_call" | custom-call | tf_op jit(solution)/shard_map/pallas_call | solution.py:580
Async XLA Ops:
  0.6 38.2 %copy-start.3 = (f32[3,3,256]{2,1,0:T(4,128)S(1)}, f32[3,3,256]{2,1,0:T(4,128)}, u32[]{:S(2)}) copy-start(f32[3,3,256]{2,1,0:T(4,128)} %taps.1) | copy-start | bytes 27652
  0.6 38.2 %copy-start.4 = (f32[256]{0:T(256)S(1)}, f32[256]{0:T(256)}, u32[]{:S(2)}) copy-start(f32[256]{0:T(256)} %param.13) | copy-start | bytes 3076
  0.7 38.2 %copy-start = (f32[512,256]{1,0:T(8,128)S(1)}, f32[512,256]{1,0:T(8,128)}, u32[]{:S(2)}) copy-start(f32[512,256]{1,0:T(8,128)} %centers.1) | copy-start | bytes 1572868
  0.7 38.2 %copy-start.2 = (f32[256,256]{1,0:T(8,128)S(1)}, f32[256,256]{1,0:T(8,128)}, u32[]{:S(2)}) copy-start(f32[256,256]{1,0:T(8,128)} %key_weight.1) | copy-start | bytes 786436
  0.7 38.2 %copy-start.1 = (f32[256,256]{1,0:T(8,128)S(1)}, f32[256,256]{1,0:T(8,128)}, u32[]{:S(2)}) copy-start(f32[256,256]{1,0:T(8,128)} %value_weight.1) | copy-start | bytes 786436
